TPU v7x, 32 devices: a whole 2x2x4 slice. The times are simulated.
32 devices in a mesh: dp: 8 (over z, y), seq: 4 (over x, core).
Axes of the slice: x: 2, y: 2, z: 4, core: 2. Of those that a mesh axis runs over, the one named last changes fastest.
Arguments:
- image_counts: int32 [8], P('dp'), may hold values from 1 to 12, as said below
- patches: bfloat16 [196, 96, 768], P(None, 'dp', 'seq'), may hold values from -6 to 6
- ln1_gain: float32 [768], P('seq'), may hold values from 0.1 to 1.9
- ln1_bias: float32 [768], P('seq'), may hold values from -1.5 to 1.5
- tok_in_weight: bfloat16 [384, 196], replicated, may hold values from -0.4375 to 0.4375
- tok_in_bias: float32 [384], replicated, may hold values from -2.5 to 2.5
- tok_out_weight: bfloat16 [196, 384], replicated, may hold values from -0.3125 to 0.3125
- tok_out_bias: float32 [196], replicated, may hold values from -2.5 to 2.5
- ln2_gain: float32 [768], P('seq'), may hold values from 0.1 to 1.9
- ln2_bias: float32 [768], P('seq'), may hold values from -1.5 to 1.5
- chan_in_weight: bfloat16 [768, 3072], P(None, 'seq'), may hold values from -0.21875 to 0.21875
- chan_in_bias: float32 [3072], P('seq'), may hold values from -2.5 to 2.5
- chan_out_weight: bfloat16 [3072, 768], P('seq'), may hold values from -0.109375 to 0.109375
- chan_out_bias: float32 [768], P('seq'), may hold values from -1.5 to 1.5
- cotangent: bfloat16 [196, 96, 768], P(None, 'dp', 'seq'), may hold values from -6 to 6
Outputs:
- mixed: bfloat16 [196, 96, 768], P(None, 'dp', 'seq')
- input_grad: bfloat16 [196, 96, 768], P(None, 'dp', 'seq')
- grad_ln1_gain: float32 [768], P('seq')
- grad_ln1_bias: float32 [768], P('seq')
- grad_tok_in: float32 [384, 196], replicated
- grad_tok_in_bias: float32 [384], replicated
- grad_tok_out: float32 [196, 384], replicated
- grad_tok_out_bias: float32 [196], replicated
- grad_ln2_gain: float32 [768], P('seq')
- grad_ln2_bias: float32 [768], P('seq')
- grad_chan_in: float32 [768, 3072], P(None, 'seq')
- grad_chan_in_bias: float32 [3072], P('seq')
- grad_chan_out: float32 [3072, 768], P('seq')
- grad_chan_out_bias: float32 [768], P('seq')
Inputs may be any that keep to these rules, and one draw needn't show every extreme that they name: `image_counts`: each entry is at least 1 and at most 12; some index of dp has all 12 slots in use.
All inputs are finite; a program needn't handle non-finite values.
Results may differ from a plain program's by a relative error of at most 0.012.
Values may be sent and summed in bfloat16 or wider, within the bound.
A program may use at most 192 MiB of HBM per device.

v0:
```python
import jax
import jax.numpy as jnp
from jax import lax
from jax.sharding import PartitionSpec as P

D = 768


def feature_sum(values):
    return lax.psum(jnp.sum(values, axis=-1, keepdims=True), "seq")


def split_norm(values, gain, shift):
    mean = feature_sum(values) / D
    centred = values - mean
    spread = feature_sum(centred * centred) / D
    inverse = lax.rsqrt(spread + 1e-06)
    scaled = centred * inverse
    return (scaled * gain + shift, scaled, inverse)


def split_norm_back(grad_normed, scaled, inverse, gain):
    grad_gain = jnp.sum(grad_normed * scaled, axis=(0, 1))
    grad_shift = jnp.sum(grad_normed, axis=(0, 1))
    weighted = grad_normed * gain
    sums = lax.psum(
        (
            jnp.sum(weighted, axis=-1, keepdims=True),
            jnp.sum(weighted * scaled, axis=-1, keepdims=True),
        ),
        "seq",
    )
    grad_values = inverse * (weighted - sums[0] / D - scaled * (sums[1] / D))
    return (grad_values, grad_gain, grad_shift)


def gelu_back(pre, grad):
    return jax.vjp(jax.nn.gelu, pre)[1](grad)[0]


def channel_hidden(rows, w_in, b_in):
    hidden_pre = jnp.einsum("pbc,ch->pbh", rows, w_in, preferred_element_type=jnp.float32) + b_in
    return (hidden_pre, jax.nn.gelu(hidden_pre).astype(jnp.bfloat16))


def per_device(
    image_counts,
    patches,
    ln1_gain,
    ln1_bias,
    tok_in_weight,
    tok_in_bias,
    tok_out_weight,
    tok_out_bias,
    ln2_gain,
    ln2_bias,
    chan_in_weight,
    chan_in_bias,
    chan_out_weight,
    chan_out_bias,
    cotangent,
):
    batch = patches.shape[1]
    valid = (jnp.arange(batch, dtype=jnp.int32) < image_counts[0]).astype(jnp.float32)
    slot_mask = valid[None, :, None]
    inputs = patches.astype(jnp.float32)
    normed_full, scaled_one, inverse_one = split_norm(inputs, ln1_gain, ln1_bias)
    normed_one = normed_full.astype(jnp.bfloat16)
    token_pre = (
        jnp.einsum("jp,pbc->jbc", tok_in_weight, normed_one, preferred_element_type=jnp.float32)
        + tok_in_bias[:, None, None]
    )
    token_act = jax.nn.gelu(token_pre).astype(jnp.bfloat16)
    token_out = (
        jnp.einsum("pj,jbc->pbc", tok_out_weight, token_act, preferred_element_type=jnp.float32)
        + tok_out_bias[:, None, None]
    )
    middle = inputs + token_out
    normed_mid, scaled_two, inverse_two = split_norm(middle, ln2_gain, ln2_bias)
    normed_two = normed_mid.astype(jnp.bfloat16)
    grad_out = cotangent.astype(jnp.float32) * slot_mask
    grad_low = grad_out.astype(jnp.bfloat16)
    grad_chan_out_bias = jnp.sum(grad_out, axis=(0, 1))
    all_normed_two = lax.all_gather(normed_two, "seq", axis=2, tiled=True)
    hidden_pre, hidden_act = channel_hidden(all_normed_two, chan_in_weight, chan_in_bias)
    partial_out = jnp.einsum(
        "pbh,hc->pbc", hidden_act, chan_out_weight, preferred_element_type=jnp.float32
    )
    chan_out = (
        lax.psum_scatter(
            partial_out.astype(jnp.bfloat16), "seq", scatter_dimension=2, tiled=True
        ).astype(jnp.float32)
        + chan_out_bias
    )
    result = (slot_mask * (middle + chan_out)).astype(jnp.bfloat16)
    all_grad = lax.all_gather(grad_low, "seq", axis=2, tiled=True)
    grad_chan_out = jnp.einsum(
        "pbh,pbc->hc", hidden_act, all_grad, preferred_element_type=jnp.float32
    )
    grad_hidden_act = jnp.einsum(
        "pbc,hc->pbh", all_grad, chan_out_weight, preferred_element_type=jnp.float32
    )
    grad_hidden = gelu_back(hidden_pre, grad_hidden_act).astype(jnp.bfloat16)
    grad_chan_in_bias = jnp.sum(grad_hidden, axis=(0, 1), dtype=jnp.float32)
    grad_chan_in = jnp.einsum(
        "pbc,pbh->ch", all_normed_two, grad_hidden, preferred_element_type=jnp.float32
    )
    partial_back = jnp.einsum(
        "pbh,ch->pbc", grad_hidden, chan_in_weight, preferred_element_type=jnp.float32
    )
    grad_normed_two = lax.psum_scatter(
        partial_back.astype(jnp.bfloat16), "seq", scatter_dimension=2, tiled=True
    ).astype(jnp.float32)
    grad_mid_norm, grad_ln2_gain, grad_ln2_bias = split_norm_back(
        grad_normed_two, scaled_two, inverse_two, ln2_gain
    )
    grad_middle = grad_out + grad_mid_norm
    grad_token_out = grad_middle.astype(jnp.bfloat16)
    grad_tok_out_bias = jnp.sum(grad_token_out, axis=(1, 2), dtype=jnp.float32)
    grad_tok_out = jnp.einsum(
        "pbc,jbc->pj", grad_token_out, token_act, preferred_element_type=jnp.float32
    )
    grad_token_act = jnp.einsum(
        "pj,pbc->jbc", tok_out_weight, grad_token_out, preferred_element_type=jnp.float32
    )
    grad_token_pre = gelu_back(token_pre, grad_token_act).astype(jnp.bfloat16)
    grad_tok_in_bias = jnp.sum(grad_token_pre, axis=(1, 2), dtype=jnp.float32)
    grad_tok_in = jnp.einsum(
        "jbc,pbc->jp", grad_token_pre, normed_one, preferred_element_type=jnp.float32
    )
    grad_normed_one = jnp.einsum(
        "jp,jbc->pbc", tok_in_weight, grad_token_pre, preferred_element_type=jnp.float32
    )
    grad_in_norm, grad_ln1_gain, grad_ln1_bias = split_norm_back(
        grad_normed_one, scaled_one, inverse_one, ln1_gain
    )
    grad_inputs = (grad_middle + grad_in_norm).astype(jnp.bfloat16)
    token_sums = lax.psum(
        (grad_tok_in, grad_tok_in_bias, grad_tok_out, grad_tok_out_bias), ("dp", "seq")
    )
    summed = lax.psum(
        (
            grad_ln1_gain,
            grad_ln1_bias,
            grad_ln2_gain,
            grad_ln2_bias,
            grad_chan_in,
            grad_chan_in_bias,
            grad_chan_out,
            grad_chan_out_bias,
        ),
        "dp",
    )
    return (
        result,
        grad_inputs,
        summed[0],
        summed[1],
        token_sums[0],
        token_sums[1],
        token_sums[2],
        token_sums[3],
        summed[2],
        summed[3],
        summed[4],
        summed[5],
        summed[6],
        summed[7],
    )


def solution(mesh):
    in_specs = (
        P("dp"),
        P(None, "dp", "seq"),
        P("seq"),
        P("seq"),
        P(),
        P(),
        P(),
        P(),
        P("seq"),
        P("seq"),
        P(None, "seq"),
        P("seq"),
        P("seq", None),
        P("seq"),
        P(None, "dp", "seq"),
    )
    out_specs = (
        P(None, "dp", "seq"),
        P(None, "dp", "seq"),
        P("seq"),
        P("seq"),
        P(),
        P(),
        P(),
        P(),
        P("seq"),
        P("seq"),
        P(None, "seq"),
        P("seq"),
        P("seq", None),
        P("seq"),
    )
    return jax.shard_map(
        per_device, mesh=mesh, in_specs=in_specs, out_specs=out_specs, check_vma=False
    )
```

profile of v0, /device:TPU:0, one launch (start us, length us, event | category | flops | bytes accessed | tf_op | source)
XLA Modules:
  0.0 583.8 jit_solution(11917940261531674464)
XLA Ops:
  7.2 0.0 copy-start
  7.2 0.0 copy-start.2
  7.2 0.0 all-gather.3.cloned.1.call-start
  7.3 1.6 convert_reduce_fusion.3
  8.9 12.7 %psum.140 = f32[196,12,1]{0,1,2:T(8,128)S(1)} all-reduce(f32[196,12,1]{0,1,2:T(8,128)S(1)} %bitcast.112), channel_id=1, replica_groups=mesh['dp'=8,'seq'=4] {'seq'}, use_global_device_ids=true, to_apply=%region_1.0 | all-reduce | flops 2352 | bytes 18816 | tf_op jit(solution)/shard_map/psum | solution.py:10
  21.6 1.6 fusion.35
  23.2 10.1 %psum.141 = f32[196,12,1]{0,1,2:T(8,128)S(1)} all-reduce(f32[196,12,1]{0,1,2:T(8,128)S(1)} %bitcast.113), channel_id=1, replica_groups=mesh['dp'=8,'seq'=4] {'seq'}, use_global_device_ids=true, to_apply=%region_3.0 | all-reduce | flops 2352 | bytes 18816 | tf_op jit(solution)/shard_map/psum | solution.py:10
  33.4 0.6 copy-done.17
  34.0 0.9 fusion.53
  34.9 0.4 copy-done.3
  35.3 1.8 fusion.62
  37.0 10.7 %psum.142 = f32[196,12,1]{0,1,2:T(8,128)} all-reduce(f32[196,12,1]{0,1,2:T(8,128)S(1)} %bitcast.119), channel_id=1, replica_groups=mesh['dp'=8,'seq'=4] {'seq'}, use_global_device_ids=true, to_apply=%region_5.0 | all-reduce | flops 2352 | bytes 18816 | tf_op jit(solution)/shard_map/psum | solution.py:10
  47.8 0.7 multiply_bitcast_fusion.4
  48.5 0.9 multiply_reduce_fusion
  49.4 11.3 %psum.143 = f32[196,12,1]{0,1,2:T(8,128)} all-reduce(f32[196,12,1]{0,1,2:T(8,128)} %bitcast.114), channel_id=1, replica_groups=mesh['dp'=8,'seq'=4] {'seq'}, use_global_device_ids=true, to_apply=%region_7.0 | all-reduce | flops 2352 | bytes 18816 | tf_op jit(solution)/shard_map/psum | solution.py:10
  60.7 0.7 rsqrt_bitcast_fusion
  61.4 0.6 copy-done.14
  62.0 2.2 add_convert_fusion
  64.3 0.0 all-gather.3.cloned.1.call-update
  64.3 0.0 all-gather.5.cloned.1.call-start
  65.0 0.5 copy-done.21
  65.5 2.8 fusion.42
  68.3 0.0 all-gather.5.cloned.1.call-update
  68.3 0.2 reduce-scatter.5.cloned.1.call-start
  68.5 33.8 %all-gather.3.cloned.1.call-done = bf16[196,12,768]{0,2,1:T(8,128)(2,1)} async-done(((bf16[196,12,192]{0,2,1:T(8,128)(2,1)}), bf16[196,12,768]{0,2,1:T(8,128)(2,1)}) %all-gather.3.cloned.1.call-update) | async-done | bytes 3612688 | tf_op jit(solution)/shard_map/all_gather | solution.py:84
  102.3 8.8 %fusion.47 = f32[196,12,768]{2,0,1:T(8,128)} fusion(bf16[196,12,768]{0,2,1:T(8,128)(2,1)} %all-gather.3.cloned.1.call-done, bf16[768,768]{1,0:T(8,128)(2,1)} %param.25), kind=kOutput, calls=%fused_computation.76 | convolution fusion | flops 2774532096 | bytes 12017664 | tf_op jit(solution)/shard_map/pbc,ch->pbh/dot_general | solution.py:42
  111.1 30.9 %all-gather.5.cloned.1.call-done = bf16[196,12,768]{0,2,1:T(8,128)(2,1)} async-done(((bf16[196,12,192]{0,2,1:T(8,128)(2,1)}), bf16[196,12,768]{0,2,1:T(8,128)(2,1)}) %all-gather.5.cloned.1.call-update) | async-done | bytes 3612688 | tf_op jit(solution)/shard_map/all_gather | solution.py:96
  142.0 11.9 %convert_reduce_fusion = (f32[768]{0:T(1024)}, bf16[196,12,768]{2,0,1:T(8,128)(2,1)S(1)}) fusion(f32[196,12,768]{2,0,1:T(8,128)} %fusion.47, f32[768]{0:T(1024)} %param.26, bf16[196,12,768]{0,2,1:T(8,128)(2,1)} %all-gather.5.cloned.1.call-done, bf16[768,768]{1,0:T(8,128)(2,1)S(1)} %copy-done), kind=kOutput, calls=%fused_computation.9 | convolution fusion | flops 2816077056 | bytes 15636480 | tf_op jit(solution)/shard_map/pbc,hc->pbh/dot_general | solution.py:100
  153.8 1.8 copy-done.32
  155.7 5.5 convolution_convert_fusion
  161.1 0.0 reduce-scatter.5.cloned.1.call-update
  161.2 0.0 reduce-scatter.3.cloned.1.call-start
  161.2 9.9 %convolution_convert_fusion.1 = bf16[196,12,768]{0,2,1:T(8,128)(2,1)} fusion(bf16[768,768]{1,0:T(8,128)(2,1)S(1)} %copy-done, f32[196,12,768]{2,0,1:T(8,128)} %fusion.47, f32[768]{0:T(1024)} %param.26), kind=kOutput, calls=%fused_computation.38 | convolution fusion | flops 2794401792 | bytes 12020736 | tf_op jit(solution)/shard_map/pbh,hc->pbc/dot_general | solution.py:86
  171.1 0.0 reduce-scatter.3.cloned.1.call-update
  171.2 0.3 all-reduce.11.cloned.1.call-start
  171.4 8.6 %convolution_bitcast_fusion.1 = f32[768,768]{1,0:T(8,128)} fusion(bf16[196,12,768]{0,2,1:T(8,128)(2,1)} %all-gather.3.cloned.1.call-done, bf16[196,12,768]{2,0,1:T(8,128)(2,1)} %copy-done.32), kind=kOutput, calls=%fused_computation.70 | convolution fusion | flops 2774532096 | bytes 9584640 | tf_op jit(solution)/shard_map/pbc,pbh->ch/dot_general | solution.py:105
  180.0 12.5 %convolution_bitcast_fusion = f32[768,768]{1,0:T(8,128)} fusion(bf16[196,12,768]{0,2,1:T(8,128)(2,1)} %all-gather.5.cloned.1.call-done, f32[196,12,768]{2,0,1:T(8,128)} %fusion.47, f32[768]{0:T(1024)S(1)} %copy-done.26), kind=kOutput, calls=%fused_computation.69 | convolution fusion | flops 2792595456 | bytes 13200384 | tf_op jit(solution)/shard_map/pbh,pbc->hc/dot_general | solution.py:97
  192.5 0.0 all-reduce.11.cloned.1.call-update
  192.6 0.0 all-reduce.9.cloned.1.call-start
  192.6 16.5 %reduce-scatter.5.cloned.1.call-done = bf16[196,12,192]{0,2,1:T(8,128)(2,1)} async-done(((bf16[196,12,768]{0,2,1:T(8,128)(2,1)}), bf16[196,12,192]{0,2,1:T(8,128)(2,1)}) %reduce-scatter.5.cloned.1.call-update) | async-done | bytes 903184 | tf_op jit(solution)/shard_map/reduce_scatter | solution.py:111
  209.1 3.6 fusion.40
  212.8 11.7 %all-reduce.5 = (f32[196,12,1]{0,1,2:T(8,128)}, f32[196,12,1]{0,1,2:T(8,128)}) all-reduce(f32[196,12,1]{0,1,2:T(8,128)} %bitcast.115, f32[196,12,1]{0,1,2:T(8,128)} %bitcast.116), channel_id=1, replica_groups=mesh['dp'=8,'seq'=4] {'seq'}, use_global_device_ids=true, to_apply=%region_13.0 | all-reduce | flops 4704 | bytes 37632 | tf_op jit(solution)/shard_map/psum | solution.py:26
  224.5 1.3 multiply_bitcast_fusion.2
  225.8 33.8 %reduce-scatter.3.cloned.1.call-done = bf16[196,12,192]{0,2,1:T(8,128)(2,1)} async-done(((bf16[196,12,768]{0,2,1:T(8,128)(2,1)}), bf16[196,12,192]{0,2,1:T(8,128)(2,1)}) %reduce-scatter.3.cloned.1.call-update) | async-done | bytes 903184 | tf_op jit(solution)/shard_map/reduce_scatter | solution.py:90
  259.6 5.1 convert_reduce_fusion.4
  264.8 3.6 convert_reduce_fusion.1
  268.4 1.8 fusion.34
  270.2 0.8 reduce_sum.153
  271.0 43.6 %all-reduce = (f32[384]{0:T(512)}, f32[196]{0:T(256)}) all-reduce(f32[384]{0:T(512)} %get-tuple-element.46, f32[196]{0:T(256)} %get-tuple-element.37), channel_id=1, replica_groups=mesh['dp'=8,'seq'=4] {'dp','seq'}, use_global_device_ids=true, to_apply=%region_24.0 | all-reduce | flops 580 | bytes 4640 | tf_op jit(solution)/shard_map/psum | solution.py:138
  314.7 12.6 %all-reduce.4 = (f32[196,12,1]{0,1,2:T(8,128)}, f32[196,12,1]{0,1,2:T(8,128)}) all-reduce(f32[196,12,1]{0,1,2:T(8,128)} %bitcast.117, f32[196,12,1]{0,1,2:T(8,128)} %bitcast.118), channel_id=1, replica_groups=mesh['dp'=8,'seq'=4] {'seq'}, use_global_device_ids=true, to_apply=%region_17.0 | all-reduce | flops 4704 | bytes 37632 | tf_op jit(solution)/shard_map/psum | solution.py:26
  327.2 1.3 multiply_bitcast_fusion
  328.5 1.3 multiply_bitcast_fusion.1
  329.9 3.3 convolution_bitcast_fusion.3
  333.1 0.1 copy-done.10
  333.2 2.3 convolution_bitcast_fusion.2
  335.5 0.0 all-reduce.9.cloned.1.call-update
  335.5 23.2 %all-reduce.2 = (f32[192]{0:T(256)}, f32[192]{0:T(256)}, f32[192]{0:T(256)}, f32[192]{0:T(256)}, f32[768]{0:T(1024)}, /*index=5*/f32[192]{0:T(256)}) all-reduce(f32[192]{0:T(256)} %get-tuple-element.16, f32[192]{0:T(256)} %reduce_sum.153, f32[192]{0:T(256)} %get-tuple-element.14, ...), channel_id=1, replica_groups=mesh['dp'=8,'seq'=4] {'dp'}, use_global_device_ids=true, to_apply=%region_19.0 | all-reduce | flops 1728 | bytes 13824 | tf_op jit(solution)/shard_map/psum | solution.py:141
  358.7 3.5 fusion.33
  362.2 73.3 %all-reduce.11.cloned.1.call-done = (f32[768,768]{1,0:T(8,128)}, f32[768,768]{1,0:T(8,128)}) async-done(((f32[768,768]{1,0:T(8,128)}, f32[768,768]{1,0:T(8,128)}), (f32[768,768]{1,0:T(8,128)}, f32[768,768]{1,0:T(8,128)})) %all-reduce.11.cloned.1.call-update) | async-done | bytes 4718608 | tf_op jit(solution)/shard_map/psum | solution.py:141
  435.5 132.7 %all-reduce.9.cloned.1.call-done = (f32[384,196]{0,1:T(8,128)}, f32[196,384]{1,0:T(8,128)}) async-done(((f32[384,196]{0,1:T(8,128)}, f32[196,384]{1,0:T(8,128)}), (f32[384,196]{0,1:T(8,128)}, f32[196,384]{1,0:T(8,128)})) %all-reduce.9.cloned.1.call-update) | async-done | bytes 602128 | tf_op jit(solution)/shard_map/psum | solution.py:138
  568.3 1.7 copy.37
  570.0 1.7 copy.38
  571.7 3.4 copy.39
  575.1 1.4 copy.40
  (61 shorter events, 0.2 us)
Async XLA Ops:
  7.2 134.8 %copy-start = (bf16[768,768]{1,0:T(8,128)(2,1)S(1)}, bf16[768,768]{1,0:T(8,128)(2,1)}, u32[]{:S(2)}) copy-start(bf16[768,768]{1,0:T(8,128)(2,1)} %param.27) | copy-start | bytes 3538948
  7.2 26.8 %copy-start.2 = (bf16[196,12,192]{0,2,1:T(8,128)(2,1)S(1)}, bf16[196,12,192]{0,2,1:T(8,128)(2,1)}, u32[]{:S(2)}) copy-start(bf16[196,12,192]{0,2,1:T(8,128)(2,1)} %param.16) | copy-start | bytes 2709508
  7.2 26.8 %copy-start.19 = (f32[192]{0:T(256)S(1)}, f32[192]{0:T(256)}, u32[]{:S(2)}) copy-start(f32[192]{0:T(256)} %param.17) | copy-start | bytes 2308
  7.2 26.8 %copy-start.15 = (bf16[384,196]{0,1:T(8,128)(2,1)S(1)}, bf16[384,196]{0,1:T(8,128)(2,1)}, u32[]{:S(2)}) copy-start(bf16[384,196]{0,1:T(8,128)(2,1)} %param.19) | copy-start | bytes 451588
  7.2 26.8 %copy-start.22 = (f32[192]{0:T(256)S(1)}, f32[192]{0:T(256)}, u32[]{:S(2)}) copy-start(f32[192]{0:T(256)} %param.18) | copy-start | bytes 2308
  7.2 95.1 %all-gather.3.cloned.1.call-start = ((), (), s32[]{:S(2)}) async-start(), calls=%async_computation.2 | async-start | bytes 5898240 | tf_op jit(solution)/shard_map/all_gather | solution.py:84
  21.6 11.8 %copy-start.12 = (f32[196,12]{0,1:T(8,128)}, f32[196,12]{0,1:T(8,128)S(1)}, u32[]{:S(2)}) copy-start(f32[196,12]{0,1:T(8,128)S(1)} %multiply_bitcast_fusion.5) | copy-start | bytes 28228
  33.4 0.6 copy-start.17
  34.0 1.3 copy-start.3
  34.0 1.3 copy-start.24
  34.0 1.3 copy-start.27
  34.0 1.2 copy-start.30
  35.3 1.8 copy-start.8
  61.4 0.6 copy-start.14
  64.3 77.7 %all-gather.5.cloned.1.call-start = ((), (), s32[]{:S(2)}) async-start(), calls=%async_computation.4 | async-start | bytes 5898240 | tf_op jit(solution)/shard_map/all_gather | solution.py:96
  65.0 0.5 copy-start.21
  68.3 140.8 %reduce-scatter.5.cloned.1.call-start = ((), (), s32[]{:S(2)}) async-start(), calls=%async_computation.5 | async-start | bytes 5898240 | tf_op jit(solution)/shard_map/reduce_scatter | solution.py:111
  142.0 13.7 %copy-start.23 = (bf16[768,768]{1,0:T(8,128)(2,1)S(1)}, bf16[768,768]{1,0:T(8,128)(2,1)}, u32[]{:S(2)}) copy-start(bf16[768,768]{1,0:T(8,128)(2,1)} %param.25) | copy-start | bytes 3538948
  153.8 1.8 copy-start.32
  161.2 98.4 %reduce-scatter.3.cloned.1.call-start = ((), (), s32[]{:S(2)}) async-start(), calls=%async_computation.3 | async-start | bytes 5898240 | tf_op jit(solution)/shard_map/reduce_scatter | solution.py:90
  171.2 8.9 %copy-start.26 = (f32[768]{0:T(1024)S(1)}, f32[768]{0:T(1024)}, u32[]{:S(2)}) copy-start(f32[768]{0:T(1024)} %param.26) | copy-start | bytes 9220
  171.2 264.4 %all-reduce.11.cloned.1.call-start = ((), (), s32[]{:S(2)}) async-start(), calls=%async_computation.7 | async-start | bytes 9437184 | tf_op jit(solution)/shard_map/psum | solution.py:141
  192.6 67.0 %copy-start.7 = (bf16[196,12,192]{0,2,1:T(8,128)(2,1)S(1)}, bf16[196,12,192]{0,2,1:T(8,128)(2,1)}, u32[]{:S(2)}) copy-start(bf16[196,12,192]{0,2,1:T(8,128)(2,1)} %param.29) | copy-start | bytes 2709508
  192.6 375.7 %all-reduce.9.cloned.1.call-start = ((), (), s32[]{:S(2)}) async-start(), calls=%async_computation.6 | async-start | bytes 1228800 | tf_op jit(solution)/shard_map/psum | solution.py:138
  259.6 5.1 copy-start.9
  259.6 5.1 copy-start.25
  259.6 5.1 copy-start.28
  264.7 3.7 copy-start.5
  264.7 3.7 copy-start.4
  264.7 3.7 copy-start.13
  264.7 3.7 copy-start.16
  264.7 3.7 copy-start.18
  264.7 3.7 copy-start.20
  268.4 1.9 copy-start.31
  329.8 3.3 copy-start.6
  329.8 3.3 copy-start.10
  329.9 3.3 copy-start.29
  571.7 3.4 copy-start.11
  571.7 4.8 copy-start.1
Sparse Core Ops, SparseCore 0:
  64.4 37.8 all-gather.2
  104.5 37.4 all-gather.4
  161.3 47.8 reduce-scatter.4
  211.7 47.8 reduce-scatter.2
  263.6 171.8 all-reduce.10
  441.3 126.9 all-reduce.8
where the time goes:
time: 590 us; the launch traced here: 584 us
  waiting for transfers between devices  321 us (54%)
  blocking collectives  136 us (23%)
  matrix products  70.8 us (12%)
  other arithmetic  27.6 us (5%)
  between operations  15.5 us (3%)
  local copies, waits for them, and re-layouts  12.3 us (2%)
    psum x1, waiting for transfers between devices, per_device(): lax.psum((grad_tok_in, grad_tok_in_bias, grad_tok_out, grad_tok_out_bias)...  133 us
    psum x1, waiting for transfers between devices, per_device(): lax.psum((grad_ln1_gain, grad_ln1_bias, grad_ln2_gain, grad_ln2_bias, gra...  73.3 us
    psum x4, blocking collectives, feature_sum(): return lax.psum(jnp.sum(values, axis=-1, keepdims=True), 'seq')  44.8 us
    psum x1, blocking collectives, per_device(): lax.psum((grad_tok_in, grad_tok_in_bias, grad_tok_out, grad_tok_out_bias)...  43.6 us
    all_gather x1, waiting for transfers between devices, per_device(): all_normed_two = lax.all_gather(normed_two, 'seq', axis=2, tiled=True)  33.8 us
    reduce_scatter x1, waiting for transfers between devices, per_device(): lax.psum_scatter(partial_out.astype(jnp.bfloat16), 'seq', scatter_dimensi...  33.8 us
    all_gather x1, waiting for transfers between devices, per_device(): all_grad = lax.all_gather(grad_low, 'seq', axis=2, tiled=True)  30.9 us
    psum x2, blocking collectives, split_norm_back(): lax.psum((jnp.sum(weighted, axis=-1, keepdims=True), jnp.sum(weighted * s...  24.3 us
  transfers between devices with their start and end apart: 6, of which 6 were waited for; matrix products, arithmetic and copies ran while one was open for 12% of the time, Pallas kernels for 0%

commit v1 on v0

v1 whole, which is shorter than its diff:
```python
import functools

import jax
import jax.numpy as jnp
from jax import lax
from jax.experimental import pallas as pl
from jax.experimental.pallas import tpu as pltpu
from jax.sharding import PartitionSpec as P

MESH = pl.DeviceIdType.MESH
BF = jnp.bfloat16
F32 = jnp.float32
EPS = 1e-06
GELU_A = 0.7978845608028654
GELU_B = GELU_A * 0.044715
LANE = 128


def gelu_parts(x):
    square = x * x
    tanh = jnp.tanh(x * (GELU_A + GELU_B * square))
    half = 0.5 + 0.5 * tanh
    slope = half + (0.5 * x) * (1.0 - tanh * tanh) * (GELU_A + (3.0 * GELU_B) * square)
    return x * half, slope


def dot(a, b):
    return lax.dot_general(a, b, (((1,), (0,)), ((), ())), preferred_element_type=F32)


def dot_nt(a, b):
    return lax.dot_general(a, b, (((1,), (1,)), ((), ())), preferred_element_type=F32)


def dot_tn(a, b):
    return lax.dot_general(a, b, (((0,), (0,)), ((), ())), preferred_element_type=F32)


def column(values, at):
    lanes = lax.broadcasted_iota(jnp.int32, values.shape, 1)
    return jnp.sum(jnp.where(lanes == at, values, 0.0), axis=-1, keepdims=True)


def put_columns(ref, first, second, at):
    lanes = lax.broadcasted_iota(jnp.int32, ref.shape, 1)
    ref[...] = jnp.where(lanes == at, first, jnp.where(lanes == at + 1, second, ref[...]))


def layer_kernel(
    cfg,
    patches_hbm,
    cot_hbm,
    vec_in,
    hidden_bias,
    tok_in,
    tok_in_t,
    tok_out,
    tok_out_t,
    tok_in_bias,
    tok_out_bias,
    win_hbm,
    wout_hbm,
    mixed_out,
    gin_out,
    gci_out,
    gco_out,
    tok_final,
    vec_final,
    win,
    wout,
    pwin,
    cwin,
    vwin,
    vown,
    vother,
    raw,
    ntb,
    gb,
    acts,
    ghs,
    gci,
    gco,
    cib,
    outp,
    outr,
    backp,
    backr,
    outx,
    backx,
    s2own,
    s2x,
    s1own,
    s1x,
    n1s,
    tas,
    tsl,
    mids,
    sc1s,
    sc2s,
    inv1s,
    inv2s,
    gms,
    w1s,
    gis,
    mos,
    gbuf,
    fbuf,
    rbuf,
    tg,
    tb,
    tcore,
    tcur,
    txr,
    tdp,
    trd,
    vg,
    vcore,
    vsend,
    vrd,
    sem_win_l,
    sem_p_l,
    sem_c_l,
    sem_p_w,
    sem_c_w,
    sem_v,
    sem_xp,
    sem_xc,
    sem_nt,
    sem_g,
    sem_op,
    sem_bp,
    sem_ox,
    sem_bx,
    sem_s,
    sem_mo,
    sem_gi,
    sem_mo_l,
    sem_gi_l,
    sem_rs,
    sem_ag,
    sem_out,
    sem_t,
    sem_tdp,
    sem_vdp,
):
    n_dp, bits, own, rows, half, full, hidden, toks, chunks, chunk = cfg
    d = lax.axis_index("dp")
    s = lax.axis_index("seq")
    c = s % 2
    x = s // 2
    core = (d, s + 1 - 2 * c)
    across = (d, s + 2 - 4 * x)

    def dp_bit(t):
        return (d // (1 << t)) % 2

    def dp_peer(t):
        m = 1 << t
        return (d + m - 2 * m * dp_bit(t), s)

    def remote(src, dst, sems, at, target):
        return pltpu.make_async_remote_copy(
            src_ref=src,
            dst_ref=dst,
            send_sem=sems.at[(0,) + at],
            recv_sem=sems.at[(1,) + at],
            device_id=target,
            device_id_type=MESH,
        )

    mine = pl.multiple_of(x * half, LANE)
    theirs = pl.multiple_of((1 - x) * half, LANE)
    weight_copies = [
        pltpu.make_async_copy(win_hbm.at[pl.ds(mine, half)], win.at[pl.ds(0, half)], sem_win_l.at[0]),
        pltpu.make_async_copy(win_hbm.at[pl.ds(theirs, half)], win.at[pl.ds(half, half)], sem_win_l.at[1]),
        pltpu.make_async_copy(wout_hbm.at[:, pl.ds(mine, half)], wout.at[:, pl.ds(0, half)], sem_win_l.at[2]),
        pltpu.make_async_copy(wout_hbm.at[:, pl.ds(theirs, half)], wout.at[:, pl.ds(half, half)], sem_win_l.at[3]),
    ]

    def p_local(j):
        return pltpu.make_async_copy(patches_hbm.at[c * own + j], pwin.at[c, j], sem_p_l.at[j])

    def c_local(j):
        return pltpu.make_async_copy(cot_hbm.at[c * own + j], cwin.at[c, j], sem_c_l.at[j])

    def p_swap(j):
        return remote(patches_hbm.at[(1 - c) * own + j], pwin.at[c, j], sem_p_w, (j,), core)

    def c_swap(j):
        return remote(cot_hbm.at[(1 - c) * own + j], cwin.at[c, j], sem_c_w, (j,), core)

    v_swap = remote(vec_in, vwin, sem_v, (0,), core)
    v_across = remote(vown, vother, sem_v, (1,), across)

    def p_across(j):
        return remote(raw.at[j, :, pl.ds(0, half)], raw.at[j, :, pl.ds(half, half)], sem_xp, (j,), across)

    def c_across(j):
        return remote(
            gb.at[j, pl.ds(0, rows), pl.ds(0, half)],
            gb.at[j, pl.ds(0, rows), pl.ds(half, half)],
            sem_xc,
            (j,),
            across,
        )

    def nt_share(j):
        return remote(ntb.at[j, pl.ds(0, rows)], ntb.at[j, pl.ds(rows, rows)], sem_nt, (j,), core)

    def g_share(j):
        return remote(gb.at[j, pl.ds(0, rows)], gb.at[j, pl.ds(rows, rows)], sem_g, (j,), core)

    def out_pair(j):
        return remote(outp.at[j, pl.ds(rows, rows)], outr.at[j], sem_op, (j,), core)

    def back_pair(j):
        return remote(backp.at[j, pl.ds(rows, rows)], backr.at[j], sem_bp, (j,), core)

    def out_across(j):
        return remote(outp.at[j, pl.ds(0, rows), pl.ds(half, half)], outx.at[j], sem_ox, (j,), across)

    def back_across(j):
        return remote(backp.at[j, pl.ds(0, rows), pl.ds(half, half)], backx.at[j], sem_bx, (j,), across)

    s2_across = remote(s2own, s2x, sem_s, (0,), across)
    s1_across = remote(s1own, s1x, sem_s, (1,), across)

    give = pl.multiple_of((1 - c) * LANE, LANE)
    keep = pl.multiple_of(c * LANE, LANE)

    def mixed_give(j):
        return remote(mos.at[j, :, pl.ds(give, 2 * LANE)], mixed_out.at[c * own + j], sem_mo, (j,), core)

    def gin_give(j):
        return remote(gis.at[j, :, pl.ds(give, 2 * LANE)], gin_out.at[c * own + j], sem_gi, (j,), core)

    def mixed_keep(j):
        return pltpu.make_async_copy(mos.at[j, :, pl.ds(keep, 2 * LANE)], mixed_out.at[c * own + j], sem_mo_l.at[j])

    def gin_keep(j):
        return pltpu.make_async_copy(gis.at[j, :, pl.ds(keep, 2 * LANE)], gin_out.at[c * own + j], sem_gi_l.at[j])

    def segment(k, t):
        start = k * chunk
        for u in range(t):
            start = start + dp_bit(u) * (chunk >> (u + 1))
        return start

    rb_base = []
    base = 0
    for t in range(bits):
        rb_base.append(base)
        base += chunks * (chunk >> (t + 1))

    def rs_at(k, t):
        size = chunk >> (t + 1)
        return pl.ds(pl.multiple_of(rb_base[t] + k * size, 16), size)

    def rs_send(k, t):
        size = chunk >> (t + 1)
        start = segment(k, t) + (1 - dp_bit(t)) * size
        return remote(
            gbuf.at[pl.ds(pl.multiple_of(start, 16), size)], rbuf.at[rs_at(k, t)], sem_rs, (t, k), dp_peer(t)
        )

    def rs_add(k, t, target):
        size = chunk >> (t + 1)
        at = pl.ds(pl.multiple_of(segment(k, t + 1), 16), size)
        total = gbuf[at].astype(F32) + rbuf[rs_at(k, t)].astype(F32)
        target[at] = total.astype(BF)

    def ag_send(k, t):
        size = chunk >> (t + 1)
        at = pl.ds(pl.multiple_of(segment(k, t + 1), 16), size)
        return remote(fbuf.at[at], fbuf.at[at], sem_ag, (t, k), dp_peer(t))

    t_half = tb.shape[0] // 2
    t_quarter = t_half // 2
    tc_keep = pl.multiple_of(c * t_half, 16)
    tc_give = pl.multiple_of((1 - c) * t_half, 16)
    tx_keep = pl.multiple_of(x * t_quarter, 16)
    tx_give = pl.multiple_of((1 - x) * t_quarter, 16)
    t_mine = pl.multiple_of(c * t_half + x * t_quarter, 16)
    t_core = remote(tb.at[pl.ds(tc_give, t_half)], tcore, sem_t, (0,), core)
    t_across = remote(tcur.at[pl.ds(tx_give, t_quarter)], txr, sem_t, (1,), across)
    t_back_x = remote(tok_final.at[pl.ds(t_mine, t_quarter)], tok_final.at[pl.ds(t_mine, t_quarter)], sem_t, (2,), across)
    t_back_c = remote(tok_final.at[pl.ds(tc_keep, t_half)], tok_final.at[pl.ds(tc_keep, t_half)], sem_t, (3,), core)
    v_core = remote(vg.at[pl.ds(0, 8)], vcore, sem_t, (4,), core)

    def t_dp(t):
        return remote(tdp.at[t], trd.at[t], sem_tdp, (t,), dp_peer(t))

    def v_dp(t):
        return remote(vsend.at[t], vrd.at[t], sem_vdp, (t,), dp_peer(t))

    barrier = pltpu.get_barrier_semaphore()
    peers = [core, across] + [dp_peer(t) for t in range(bits)]
    for peer in peers:
        pl.semaphore_signal(barrier, inc=1, device_id=peer, device_id_type=MESH)
    pl.semaphore_wait(barrier, len(peers))

    def start_windows(j, carry):
        p_swap(j).start()
        p_local(j).start()
        c_swap(j).start()
        c_local(j).start()
        return carry

    v_swap.start()
    lax.fori_loop(0, own, start_windows, 0)
    for copy in weight_copies:
        copy.start()

    gci[...] = jnp.zeros_like(gci)
    gco[...] = jnp.zeros_like(gco)
    cib[...] = jnp.zeros_like(cib)
    tg[...] = jnp.zeros_like(tg)
    vg[...] = jnp.zeros_like(vg)
    s2own[...] = jnp.zeros_like(s2own)
    s1own[...] = jnp.zeros_like(s1own)

    def merge(first, second):
        middle = first[:, LANE:].astype(F32) + second[:, :LANE].astype(F32)
        return first[:, :LANE], middle.astype(first.dtype), second[:, LANE:]

    def merge_send(j):
        p_swap(j).wait_recv()
        p_local(j).wait()
        for at, part in enumerate(merge(pwin[0, j], pwin[1, j])):
            raw[j, :, pl.ds(at * LANE, LANE)] = part
        p_across(j).start()
        c_swap(j).wait_recv()
        c_local(j).wait()
        for at, part in enumerate(merge(cwin[0, j], cwin[1, j])):
            gb[j, pl.ds(0, rows), pl.ds(at * LANE, LANE)] = part
        c_across(j).start()

    merge_send(0)
    v_swap.wait_recv()
    vmine = vec_in[...]
    vpart = vwin[...]
    v0 = jnp.where(c == 0, vmine, vpart)
    v1 = jnp.where(c == 0, vpart, vmine)
    vown[:, pl.ds(0, LANE)] = v0[:, :LANE]
    vown[:, pl.ds(LANE, LANE)] = v0[:, LANE:] + v1[:, :LANE]
    vown[:, pl.ds(2 * LANE, LANE)] = v1[:, LANE:]
    v_across.start()
    merge_send(1)
    v_across.wait_recv()

    def vector(row):
        return jnp.concatenate([vown[pl.ds(row, 1), :], vother[pl.ds(row, 1), :]], axis=1)

    def token_forward(j):
        values = raw[j].astype(F32)
        mean = jnp.sum(values, axis=-1, keepdims=True) * (1.0 / full)
        centred = values - mean
        inverse = lax.rsqrt(jnp.sum(centred * centred, axis=-1, keepdims=True) * (1.0 / full) + EPS)
        scaled = centred * inverse
        normed = (scaled * vector(0) + vector(1)).astype(BF)
        sc1s[j] = scaled[:, :half].astype(BF)
        inv1s[j] = inverse
        n1s[j] = normed[:, :half]
        act, slope = gelu_parts(dot(tok_in[...], normed) + tok_in_bias[...])
        act = act.astype(BF)
        tas[j] = act[:, :half]
        tsl[j] = slope[:, :half].astype(BF)
        middle = values + (dot(tok_out[...], act) + tok_out_bias[...])
        mids[j] = middle[:, :half]
        mean = jnp.sum(middle, axis=-1, keepdims=True) * (1.0 / full)
        centred = middle - mean
        inverse = lax.rsqrt(jnp.sum(centred * centred, axis=-1, keepdims=True) * (1.0 / full) + EPS)
        scaled = centred * inverse
        sc2s[j] = scaled[:, :half].astype(BF)
        inv2s[j] = inverse
        ntb[j, pl.ds(0, rows)] = (scaled * vector(2) + vector(3)).astype(BF)

    def channel(j):
        nt = ntb[j]
        g = gb[j]
        width = 256
        for at in range(hidden // width):
            cols = pl.ds(at * width, width)
            pre = dot(nt, win[:, cols]) + hidden_bias[:, cols]
            back = dot_nt(g, wout[cols, :])
            act, slope = gelu_parts(pre)
            acts[:, cols] = act.astype(BF)
            grad = (slope * back).astype(BF)
            ghs[:, cols] = grad
            cib[:, cols] += jnp.sum(grad.astype(F32), axis=0, keepdims=True)
        backp[j] = dot_nt(ghs[...], win[...]).astype(BF)
        back_pair(j).start()
        outp[j] = dot(acts[...], wout[...]).astype(BF)
        out_pair(j).start()
        gco[...] += dot_tn(acts[...], g)
        gci[...] += dot_tn(nt, ghs[...])

    def phase_a(j, carry):
        @pl.when(j + 2 < own)
        def _():
            merge_send(j + 2)

        @pl.when(j < own)
        def _():
            p_across(j).wait_recv()
            token_forward(j)
            nt_share(j).start()
            c_across(j).wait_recv()
            g_share(j).start()

        @pl.when(j == 0)
        def _():
            for copy in weight_copies:
                copy.wait()

        @pl.when(j > 0)
        def _():
            nt_share(j - 1).wait_recv()
            g_share(j - 1).wait_recv()
            channel(j - 1)

        return carry

    lax.fori_loop(0, own + 1, phase_a, 0)

    tiles = hidden // LANE
    for at in range(tiles):
        gbuf[pl.ds(at * full, full)] = gci[:, pl.ds(at * LANE, LANE)].astype(BF)
    for at in range(full // LANE):
        gbuf[pl.ds(tiles * full + at * hidden, hidden)] = gco[:, pl.ds(at * LANE, LANE)].astype(BF)

    def start_rs(k, carry):
        rs_send(k, 0).start()
        return carry

    lax.fori_loop(0, chunks, start_rs, 0)

    def pair_sums(j, carry):
        back_pair(j).wait_recv()
        total = backp[j, pl.ds(0, rows)].astype(F32) + backr[j].astype(F32)
        first = jnp.sum(total * vector(2), axis=-1, keepdims=True)
        second = jnp.sum(total * (ntb[j, pl.ds(0, rows)].astype(F32) - vector(3)), axis=-1, keepdims=True)
        put_columns(s2own, first, second, 2 * j)
        backp[j, pl.ds(0, rows)] = total.astype(BF)
        back_across(j).start()
        return carry

    lax.fori_loop(0, own, pair_sums, 0)
    s2_across.start()

    def pair_outs(j, carry):
        out_pair(j).wait_recv()
        total = outp[j, pl.ds(0, rows)].astype(F32) + outr[j].astype(F32)
        outp[j, pl.ds(0, rows)] = total.astype(BF)
        out_across(j).start()
        return carry

    lax.fori_loop(0, own, pair_outs, 0)
    s2_across.wait_recv()
    s2x[...] = (s2own[...] + s2x[...]) * (1.0 / full)

    def token_backward(j):
        back_across(j).wait_recv()
        grad_normed = backp[j, pl.ds(0, rows), pl.ds(0, half)].astype(F32) + backx[j].astype(F32)
        scaled = sc2s[j].astype(F32)
        grad_out = gb[j, pl.ds(0, rows), pl.ds(0, half)].astype(F32)
        sums = s2x[...]
        weighted = grad_normed * vown[pl.ds(2, 1), :]
        grad_mid = grad_out + inv2s[j] * (weighted - column(sums, 2 * j) - scaled * column(sums, 2 * j + 1))
        gms[j] = grad_mid
        vg[pl.ds(2, 1), :] += jnp.sum(grad_normed * scaled, axis=0, keepdims=True)
        vg[pl.ds(3, 1), :] += jnp.sum(grad_normed, axis=0, keepdims=True)
        vg[pl.ds(4, 1), :] += jnp.sum(grad_out, axis=0, keepdims=True)
        low = grad_mid.astype(BF)
        tg[pl.ds(0, rows), pl.ds(rows + 1, 1)] += jnp.sum(low.astype(F32), axis=-1, keepdims=True)
        tg[pl.ds(toks, toks), pl.ds(0, rows)] += dot_nt(tas[j], low)
        grad_pre = (tsl[j].astype(F32) * dot(tok_out_t[...], low)).astype(BF)
        tg[pl.ds(0, toks), pl.ds(rows, 1)] += jnp.sum(grad_pre.astype(F32), axis=-1, keepdims=True)
        tg[pl.ds(0, toks), pl.ds(0, rows)] += dot_nt(grad_pre, n1s[j])
        grad_one = dot(tok_in_t[...], grad_pre)
        scaled = sc1s[j].astype(F32)
        vg[pl.ds(0, 1), :] += jnp.sum(grad_one * scaled, axis=0, keepdims=True)
        vg[pl.ds(1, 1), :] += jnp.sum(grad_one, axis=0, keepdims=True)
        weighted = grad_one * vown[pl.ds(0, 1), :]
        w1s[j] = weighted
        put_columns(
            s1own,
            jnp.sum(weighted, axis=-1, keepdims=True),
            jnp.sum(weighted * scaled, axis=-1, keepdims=True),
            2 * j,
        )

    def input_grads(j, carry):
        sums = (s1own[...] + s1x[...]) * (1.0 / full)
        scaled = sc1s[j].astype(F32)
        grad = gms[j] + inv1s[j] * (w1s[j] - column(sums, 2 * j) - scaled * column(sums, 2 * j + 1))
        gis[j] = grad.astype(BF)
        gin_give(j).start()
        gin_keep(j).start()
        return carry

    def mixed_parts(j):
        out_across(j).wait_recv()
        total = outp[j, pl.ds(0, rows), pl.ds(0, half)].astype(F32) + outx[j].astype(F32)
        mos[j] = (mids[j] + (total + vown[pl.ds(4, 1), :])).astype(BF)
        mixed_give(j).start()
        mixed_keep(j).start()

    def gradient_step(i):
        for e in reversed(range(2 * bits)):
            k = i - e

            @pl.when((k >= 0) & (k < chunks))
            def _(e=e, k=k):
                if e < bits:
                    rs_send(k, e).wait_recv()
                    if e + 1 < bits:
                        rs_add(k, e, gbuf)
                        rs_send(k, e + 1).start()
                    else:
                        rs_add(k, e, fbuf)
                        ag_send(k, e).start()
                else:
                    t = 2 * bits - 1 - e
                    ag_send(k, t).wait_recv()
                    if t > 0:
                        ag_send(k, t - 1).start()

    def token_step(e):
        if e == 0:
            tb[...] = tg[...].astype(BF)
            for at in range(hidden // half):
                vg[pl.ds(8 + at, 1), :] = cib[:, pl.ds(at * half, half)]
            t_core.start()
            v_core.start()
            s1_across.start()
        elif e == 1:
            t_core.wait_recv()
            v_core.wait_recv()
            tcur[...] = (tb[pl.ds(tc_keep, t_half)].astype(F32) + tcore[...].astype(F32)).astype(BF)
            t_across.start()
            vsend[0, pl.ds(0, 8)] = vg[pl.ds(0, 8)] + vcore[...]
            vsend[0, pl.ds(8, 8)] = vg[pl.ds(8, 8)]
            v_dp(0).start()
            s1_across.wait_recv()
            lax.fori_loop(0, own, input_grads, 0)
        elif e == 2:
            t_across.wait_recv()
            tdp[0] = (tcur[pl.ds(tx_keep, t_quarter)].astype(F32) + txr[...].astype(F32)).astype(BF)
            t_dp(0).start()
        elif e < 3 + bits:
            t = e - 3
            t_dp(t).wait_recv()
            v_dp(t).wait_recv()
            total = (tdp[t].astype(F32) + trd[t].astype(F32)).astype(BF)
            vec = vsend[t] + vrd[t]
            if t + 1 < bits:
                tdp[t + 1] = total
                vsend[t + 1] = vec
                t_dp(t + 1).start()
                v_dp(t + 1).start()
            else:
                tok_final[pl.ds(t_mine, t_quarter)] = total
                vec_final[...] = vec
                t_back_x.start()
        elif e == 3 + bits:
            t_back_x.wait_recv()
            t_back_c.start()
        else:
            t_back_c.wait_recv()

    token_first = own
    token_steps = 5 + bits
    last = max(chunks + 2 * bits - 1, token_first + token_steps)

    def phase_b(i, carry):
        gradient_step(i)

        @pl.when(i < own)
        def _():
            token_backward(i)

        for e in range(token_steps):

            @pl.when(i == token_first + e)
            def _(e=e):
                token_step(e)

        @pl.when((i >= own) & (i < 2 * own))
        def _():
            mixed_parts(i - own)

        return carry

    lax.fori_loop(0, max(last, 2 * own), phase_b, 0)

    def out_copies():
        copies = []
        for at in range(tiles):
            lanes = pl.ds(at * LANE, LANE)
            for part, to in enumerate((mine, theirs)):
                copies.append(
                    pltpu.make_async_copy(
                        fbuf.at[pl.ds(at * full + part * half, half)],
                        gci_out.at[pl.ds(to, half), lanes],
                        sem_out.at[len(copies)],
                    )
                )
        for at in range(full // LANE):
            to = mine if at < half // LANE else theirs
            lanes = pl.ds(pl.multiple_of(to + (at % (half // LANE)) * LANE, LANE), LANE)
            copies.append(
                pltpu.make_async_copy(
                    fbuf.at[pl.ds(tiles * full + at * hidden, hidden)],
                    gco_out.at[:, lanes],
                    sem_out.at[len(copies)],
                )
            )
        return copies

    outs = out_copies()
    for copy in outs:
        copy.start()

    def drain(j, carry):
        for make in (
            p_swap, c_swap, p_across, c_across, nt_share, g_share, out_pair, back_pair, out_across, back_across
        ):
            make(j).wait_send()
        mixed_give(j).wait()
        gin_give(j).wait()
        mixed_keep(j).wait()
        gin_keep(j).wait()
        return carry

    lax.fori_loop(0, own, drain, 0)

    def drain_sums(k, carry):
        for t in range(bits):
            rs_send(k, t).wait_send()
            ag_send(k, t).wait_send()
        return carry

    lax.fori_loop(0, chunks, drain_sums, 0)
    for copy in [v_swap, v_across, s2_across, s1_across, t_core, t_across, t_back_x, t_back_c, v_core]:
        copy.wait_send()
    for t in range(bits):
        t_dp(t).wait_send()
        v_dp(t).wait_send()
    for copy in outs:
        copy.wait()


def run_layer(n_dp, patches, cot, vec, hidden_bias, tok_in, tok_out, tok_in_bias, tok_out_bias, win, wout):
    batch, rows, _ = patches.shape
    own = batch // 2
    full, hidden = win.shape
    half = full // 2
    toks = tok_in.shape[0]
    bits = n_dp.bit_length() - 1
    grad_rows = 2 * full * hidden // LANE
    chunks = next(k for k in (6, 9, 3, 1) if grad_rows % (k * n_dp * 16) == 0)
    chunk = grad_rows // chunks
    cfg = (n_dp, bits, own, rows, half, full, hidden, toks, chunks, chunk)
    vmem = pltpu.VMEM
    dma = pltpu.SemaphoreType.DMA
    rs_rows = sum(chunks * (chunk >> (t + 1)) for t in range(bits))
    scratch = [
        vmem((full, hidden), BF),
        vmem((hidden, full), BF),
        vmem((2, own, rows, 2 * LANE), BF),
        vmem((2, own, rows, 2 * LANE), BF),
        vmem((8, 2 * LANE), F32),
        vmem((8, half), F32),
        vmem((8, half), F32),
        vmem((own, rows, full), BF),
        vmem((own, 2 * rows, full), BF),
        vmem((own, 2 * rows, full), BF),
        vmem((2 * rows, hidden), BF),
        vmem((2 * rows, hidden), BF),
        vmem((full, hidden), F32),
        vmem((hidden, full), F32),
        vmem((1, hidden), F32),
        vmem((own, 2 * rows, full), BF),
        vmem((own, rows, full), BF),
        vmem((own, 2 * rows, full), BF),
        vmem((own, rows, full), BF),
        vmem((own, rows, half), BF),
        vmem((own, rows, half), BF),
        vmem((rows, LANE), F32),
        vmem((rows, LANE), F32),
        vmem((rows, LANE), F32),
        vmem((rows, LANE), F32),
        vmem((own, rows, half), BF),
        vmem((own, toks, half), BF),
        vmem((own, toks, half), BF),
        vmem((own, rows, half), F32),
        vmem((own, rows, half), BF),
        vmem((own, rows, half), BF),
        vmem((own, rows, 1), F32),
        vmem((own, rows, 1), F32),
        vmem((own, rows, half), F32),
        vmem((own, rows, half), F32),
        vmem((own, rows, half), BF),
        vmem((own, rows, half), BF),
        vmem((grad_rows, LANE), BF),
        vmem((grad_rows, LANE), BF),
        vmem((rs_rows, LANE), BF),
        vmem((2 * toks, 2 * LANE), F32),
        vmem((2 * toks, 2 * LANE), BF),
        vmem((toks, 2 * LANE), BF),
        vmem((toks, 2 * LANE), BF),
        vmem((toks // 2, 2 * LANE), BF),
        vmem((bits, toks // 2, 2 * LANE), BF),
        vmem((bits, toks // 2, 2 * LANE), BF),
        vmem((16, half), F32),
        vmem((8, half), F32),
        vmem((bits, 16, half), F32),
        vmem((bits, 16, half), F32),
        dma((4,)),
        dma((own,)),
        dma((own,)),
        dma((2, own)),
        dma((2, own)),
        dma((2, 2)),
        dma((2, own)),
        dma((2, own)),
        dma((2, own)),
        dma((2, own)),
        dma((2, own)),
        dma((2, own)),
        dma((2, own)),
        dma((2, own)),
        dma((2, 2)),
        dma((2, own)),
        dma((2, own)),
        dma((own,)),
        dma((own,)),
        dma((2, bits, chunks)),
        dma((2, bits, chunks)),
        dma((2 * (hidden // LANE) + full // LANE,)),
        dma((2, 5)),
        dma((2, bits)),
        dma((2, bits)),
    ]
    hbm = pl.BlockSpec(memory_space=pl.ANY)
    inside = pl.BlockSpec(memory_space=pltpu.VMEM)
    return pl.pallas_call(
        functools.partial(layer_kernel, cfg),
        out_shape=(
            jax.ShapeDtypeStruct((batch, rows, 2 * LANE), BF),
            jax.ShapeDtypeStruct((batch, rows, 2 * LANE), BF),
            jax.ShapeDtypeStruct((full, hidden), BF),
            jax.ShapeDtypeStruct((hidden, full), BF),
            jax.ShapeDtypeStruct((2 * toks, 2 * LANE), BF),
            jax.ShapeDtypeStruct((16, half), F32),
        ),
        in_specs=[hbm, hbm] + [inside] * 8 + [hbm, hbm],
        out_specs=(hbm, hbm, hbm, hbm, inside, inside),
        scratch_shapes=scratch,
        compiler_params=pltpu.CompilerParams(
            collective_id=0, has_side_effects=True, vmem_limit_bytes=63 * 2**20
        ),
        name="mixer_layer",
    )(
        patches, cot, vec, hidden_bias, tok_in, tok_in.T, tok_out, tok_out.T, tok_in_bias, tok_out_bias, win, wout
    )


def per_device(
    n_dp,
    image_counts,
    patches,
    ln1_gain,
    ln1_bias,
    tok_in_weight,
    tok_in_bias,
    tok_out_weight,
    tok_out_bias,
    ln2_gain,
    ln2_bias,
    chan_in_weight,
    chan_in_bias,
    chan_out_weight,
    chan_out_bias,
    cotangent,
):
    count, batch, width = patches.shape
    rows = -(-count // 16) * 16
    c = lax.axis_index("seq") % 2
    spare = 2 * LANE - width
    valid = jnp.arange(batch, dtype=jnp.int32) < image_counts[0]

    def window(values):
        low = [(0, 0)] * (values.ndim - 1)
        return jnp.where(c == 0, jnp.pad(values, low + [(0, spare)]), jnp.pad(values, low + [(spare, 0)]))

    def images(values):
        moved = jnp.transpose(values, (1, 0, 2))
        return window(jnp.pad(moved, ((0, 0), (0, rows - count), (0, 0))))

    masked = jnp.where(valid[None, :, None], cotangent, jnp.zeros((), BF))
    vec = window(
        jnp.concatenate(
            [
                jnp.stack([ln1_gain, ln1_bias, ln2_gain, ln2_bias, chan_out_bias]),
                jnp.zeros((3, width), F32),
            ]
        )
    )
    pad = rows - count
    mixed, gin, gci, gco, tok, vecs = run_layer(
        n_dp,
        images(patches),
        images(masked),
        vec,
        chan_in_bias[None, :],
        jnp.pad(tok_in_weight, ((0, 0), (0, pad))),
        jnp.pad(tok_out_weight, ((0, pad), (0, 0))),
        tok_in_bias[:, None],
        jnp.pad(tok_out_bias, (0, pad))[:, None],
        chan_in_weight,
        chan_out_weight,
    )

    def rows_of(values):
        return jnp.transpose(
            lax.dynamic_slice_in_dim(values[:, :count], c * spare, width, axis=2), (1, 0, 2)
        )

    toks = tok_in_weight.shape[0]
    mine = lax.dynamic_slice_in_dim(vecs[:5], c * width, width, axis=1)
    result = jnp.where(valid[None, :, None], rows_of(mixed), jnp.zeros((), BF))
    tok = tok.astype(F32)
    return (
        result,
        rows_of(gin),
        mine[0],
        mine[1],
        tok[:toks, :count],
        tok[:toks, rows],
        tok[toks:, :count].T,
        tok[:count, rows + 1],
        mine[2],
        mine[3],
        gci.astype(F32),
        vecs[8:10].reshape(-1),
        gco.astype(F32),
        mine[4],
    )


def solution(mesh):
    in_specs = (
        P("dp"),
        P(None, "dp", "seq"),
        P("seq"),
        P("seq"),
        P(),
        P(),
        P(),
        P(),
        P("seq"),
        P("seq"),
        P(None, "seq"),
        P("seq"),
        P("seq", None),
        P("seq"),
        P(None, "dp", "seq"),
    )
    out_specs = (
        P(None, "dp", "seq"),
        P(None, "dp", "seq"),
        P("seq"),
        P("seq"),
        P(),
        P(),
        P(),
        P(),
        P("seq"),
        P("seq"),
        P(None, "seq"),
        P("seq"),
        P("seq", None),
        P("seq"),
    )
    return jax.shard_map(
        functools.partial(per_device, mesh.shape["dp"]),
        mesh=mesh,
        in_specs=in_specs,
        out_specs=out_specs,
        check_vma=False,
    )
```

time: 590 us -> 185 us (0.31)
  waiting for transfers between devices: 321 us -> 0 us
  Pallas kernels: 0 us -> 155 us
  blocking collectives: 136 us -> 0 us
  matrix products: 70.8 us -> 0 us
  other arithmetic: 27.6 us -> 7.56 us
  between operations: 15.5 us -> 1.53 us
  local copies, waits for them, and re-layouts: 12.3 us -> 20 us
    psum x2 -> x0, waiting for transfers between devices: 206 us -> none  [the longest x1 133 us: per_device(): lax.psum((grad_tok_in, grad_tok_in_bias, grad_tok_out, grad_tok_out_bias)...]
    pallas_call x0 -> x1, Pallas kernels: none -> 155 us  [run_layer(): pl.pallas_call(functools.partial(layer_kernel, cfg), out_shape=(jax.Shape...]
    psum x8 -> x0, blocking collectives: 136 us -> none  [the longest x4 44.8 us: feature_sum(): return lax.psum(jnp.sum(values, axis=-1, keepdims=True), 'seq')]
    dot_general x12 -> x0, matrix products: 70.8 us -> none  [the longest x1 12.5 us: per_device(): jnp.einsum('pbh,pbc->hc', hidden_act, all_grad, preferred_element_type=jn...]
    all_gather x2 -> x0, waiting for transfers between devices: 64.7 us -> none  [the longest x1 33.8 us: per_device(): all_normed_two = lax.all_gather(normed_two, 'seq', axis=2, tiled=True)]
    reduce_scatter x2 -> x0, waiting for transfers between devices: 50.3 us -> none  [the longest x1 33.8 us: per_device(): lax.psum_scatter(partial_out.astype(jnp.bfloat16), 'seq', scatter_dimensi...]
    reduce_sum x6 -> x0, other arithmetic: 13.6 us -> none  [the longest x1 5.08 us: per_device(): grad_tok_out_bias = jnp.sum(grad_token_out, axis=(1, 2), dtype=jnp.float32)]
    unnamed x70 -> x37, local copies, waits for them, and re-layouts: 12.3 us -> 8.48 us
  transfers between devices with their start and end apart: 6 -> 0, of which waited for: 6 -> 0; matrix products, arithmetic and copies ran while one was open for 12% -> 0% of each run, Pallas kernels for 0% -> 0%
where the time goes in v1:
time: 185 us; the launch traced here: 184 us
  Pallas kernels  155 us (84%)
  local copies, waits for them, and re-layouts  20 us (11%)
  other arithmetic  7.56 us (4%)
    pallas_call x1, Pallas kernels, run_layer(): pl.pallas_call(functools.partial(layer_kernel, cfg), out_shape=(jax.Shape...  155 us
    unnamed x37, local copies, waits for them, and re-layouts  8.48 us

profile of v1, /device:TPU:0, one launch (start us, length us, event | category | flops | bytes accessed | tf_op | source)
XLA Modules:
  0.0 183.8 jit_solution(5959770329531235023)
XLA Ops:
  0.6 1.6 copy.39
  2.9 0.1 select_bitcast_fusion.1
  3.1 0.2 pad.44
  3.3 1.6 copy.38
  5.0 0.2 pad.41
  5.2 0.0 copy-start.8
  5.2 0.0 copy-start.9
  5.2 0.0 copy-start.10
  5.2 0.0 copy-start.11
  5.2 0.0 copy-start.12
  5.3 0.0 copy-start.6
  5.3 0.0 copy-start.3
  5.3 0.0 copy-start.4
  5.3 3.0 %pad_select_fusion = (bf16[12,208,256]{2,1,0:T(8,128)(2,1)}, bf16[12,208,256]{2,1,0:T(8,128)(2,1)}) fusion(bf16[12,208,192]{2,1,0:T(8,128)(2,1)S(1)} %pad.44, pred[]{:T(512)S(6)} %eq.4, bf16[12,208,192]{2,1,0:T(8,128)(2,1)S(1)} %pad.41), kind=kLoop, calls=%fused_computation | loop fusion | flops 1277952 | bytes 4472833 | tf_op jit(solution)/shard_map/jit(_where)/select_n | solution.py:796
  8.3 0.0 copy-done.8
  8.3 0.0 copy-done.9
  8.3 0.0 copy-done.10
  8.3 0.0 copy-done.11
  8.3 0.0 copy-done.12
  8.3 0.7 pad_select_fusion.2.vec_in
  9.0 0.0 copy-done.6
  9.0 0.6 broadcast_in_dim.38.hidden_bias
  9.6 0.0 copy-done.3
  9.6 0.0 copy-start.7
  9.6 0.1 copy.49
  9.7 0.0 copy-start.13
  9.8 0.7 pad.49.clone.tok_in
  10.5 0.7 pad_bitcast_fusion.tok_in_t
  11.1 0.0 copy-done.4
  11.1 0.1 copy.40
  11.3 0.1 copy.50
  11.4 0.7 pad.50.clone.tok_out
  12.2 0.7 pad_bitcast_fusion.1.tok_out_t
  12.9 0.0 copy-done.7
  12.9 0.8 broadcast_in_dim.42.tok_in_bias
  13.7 0.0 copy-done.13
  13.7 0.8 copy.44.tok_out_bias
  14.4 154.7 %mixer_layer.1 = (bf16[12,208,256]{2,1,0:T(8,128)(2,1)}, bf16[12,208,256]{2,1,0:T(8,128)(2,1)}, bf16[768,768]{1,0:T(8,128)(2,1)}, bf16[768,768]{1,0:T(8,128)(2,1...) custom-call(bf16[12,208,256]{2,1,0:T(8,128)(2,1)} %get-tuple-element.60.patches_hbm, ...), custom_call_target="tpu_custom_call" | custom-call | tf_op jit(solution)/shard_map/mixer_layer/pallas_call | solution.py:748
  169.1 1.4 slice.39
  170.5 0.5 select_bitcast_fusion
  171.1 1.5 copy.45
  172.5 1.4 slice.40
  173.9 0.5 dynamic-slice_bitcast_fusion
  174.4 0.0 copy-start.5
  174.4 0.0 copy-start
  174.4 1.5 copy.46
  175.9 0.0 copy-done.5
  175.9 0.7 fusion
  176.6 0.0 copy-done
  176.6 0.9 copy.47
  177.5 0.0 copy-start.2
  177.5 0.1 convert_element_type.28
  177.6 0.8 slice_reduce_fusion
  178.4 0.9 copy.48
  179.3 0.7 slice_reduce_fusion.1
  180.0 0.0 copy-done.2
  180.0 0.0 copy-start.1
  180.0 1.6 convert_element_type.29
  181.6 0.6 reshape.35
  182.2 0.0 copy-done.1
  182.2 1.6 convert_element_type.30
  (8 shorter events, 0.1 us)
Async XLA Ops:
  5.2 3.1 %copy-start.8 = (f32[192]{0:T(256)S(1)}, f32[192]{0:T(256)}, u32[]{:S(2)}) copy-start(f32[192]{0:T(256)} %param.17) | copy-start | bytes 2308
  5.2 3.1 %copy-start.9 = (f32[192]{0:T(256)S(1)}, f32[192]{0:T(256)}, u32[]{:S(2)}) copy-start(f32[192]{0:T(256)} %param.18) | copy-start | bytes 2308
  5.2 3.1 %copy-start.10 = (f32[192]{0:T(256)S(1)}, f32[192]{0:T(256)}, u32[]{:S(2)}) copy-start(f32[192]{0:T(256)} %param.23) | copy-start | bytes 2308
  5.2 3.1 %copy-start.11 = (f32[192]{0:T(256)S(1)}, f32[192]{0:T(256)}, u32[]{:S(2)}) copy-start(f32[192]{0:T(256)} %param.24) | copy-start | bytes 2308
  5.2 3.1 %copy-start.12 = (f32[192]{0:T(256)S(1)}, f32[192]{0:T(256)}, u32[]{:S(2)}) copy-start(f32[192]{0:T(256)} %param.28) | copy-start | bytes 2308
  5.3 3.8 %copy-start.6 = (f32[768]{0:T(1024)S(1)}, f32[768]{0:T(1024)}, u32[]{:S(2)}) copy-start(f32[768]{0:T(1024)} %param.26) | copy-start | bytes 9220
  5.3 4.3 %copy-start.3 = (bf16[384,196]{0,1:T(8,128)(2,1)S(1)}, bf16[384,196]{0,1:T(8,128)(2,1)}, u32[]{:S(2)}) copy-start(bf16[384,196]{0,1:T(8,128)(2,1)} %param.19) | copy-start | bytes 451588
  5.3 5.9 %copy-start.4 = (bf16[196,384]{1,0:T(8,128)(2,1)S(1)}, bf16[196,384]{1,0:T(8,128)(2,1)}, u32[]{:S(2)}) copy-start(bf16[196,384]{1,0:T(8,128)(2,1)} %param.21) | copy-start | bytes 451588
  9.6 3.3 %copy-start.7 = (f32[384]{0:T(512)S(1)}, f32[384]{0:T(512)}, u32[]{:S(2)}) copy-start(f32[384]{0:T(512)} %param.20) | copy-start | bytes 4612
  9.7 3.9 %copy-start.13 = (f32[196]{0:T(256)S(1)}, f32[196]{0:T(256)}, u32[]{:S(2)}) copy-start(f32[196]{0:T(256)} %param.22) | copy-start | bytes 2356
  174.4 1.5 copy-start.5
  174.4 2.2 %copy-start = (bf16[768,256]{1,0:T(8,128)(2,1)S(1)}, bf16[768,256]{1,0:T(8,128)(2,1)}, u32[]{:S(2)}) copy-start(bf16[768,256]{1,0:T(8,128)(2,1)} %get-tuple-element.23) | copy-start | bytes 1179652
  177.5 2.5 %copy-start.2 = (bf16[768,768]{1,0:T(8,128)(2,1)S(1)}, bf16[768,768]{1,0:T(8,128)(2,1)}, u32[]{:S(2)}) copy-start(bf16[768,768]{1,0:T(8,128)(2,1)} %get-tuple-element.24) | copy-start | bytes 3538948
  180.0 2.2 %copy-start.1 = (bf16[768,768]{1,0:T(8,128)(2,1)S(1)}, bf16[768,768]{1,0:T(8,128)(2,1)}, u32[]{:S(2)}) copy-start(bf16[768,768]{1,0:T(8,128)(2,1)} %get-tuple-element.25) | copy-start | bytes 3538948

commit v2 on v0

v2 whole, which is shorter than its diff:
```python
import functools

import jax
import jax.numpy as jnp
from jax import lax
from jax.experimental import pallas as pl
from jax.experimental.pallas import tpu as pltpu
from jax.sharding import PartitionSpec as P

MESH = pl.DeviceIdType.MESH
BF = jnp.bfloat16
F32 = jnp.float32
EPS = 1e-06
GELU_A = 0.7978845608028654
GELU_B = GELU_A * 0.044715
LANE = 128


def gelu_parts(x):
    square = x * x
    tanh = jnp.tanh(x * (GELU_A + GELU_B * square))
    half = 0.5 + 0.5 * tanh
    slope = half + (0.5 * x) * (1.0 - tanh * tanh) * (GELU_A + (3.0 * GELU_B) * square)
    return x * half, slope


def dot(a, b):
    return lax.dot_general(a, b, (((1,), (0,)), ((), ())), preferred_element_type=F32)


def dot_nt(a, b):
    return lax.dot_general(a, b, (((1,), (1,)), ((), ())), preferred_element_type=F32)


def dot_tn(a, b):
    return lax.dot_general(a, b, (((0,), (0,)), ((), ())), preferred_element_type=F32)


def diagonal(rows, columns):
    return lax.broadcasted_iota(jnp.int32, (rows, columns), 0) == lax.broadcasted_iota(
        jnp.int32, (rows, columns), 1
    )


def to_row(values, columns):
    return jnp.sum(jnp.where(diagonal(values.shape[0], columns), values, 0.0), axis=0, keepdims=True)


def to_column(values, rows):
    return jnp.sum(jnp.where(diagonal(rows, values.shape[1]), values, 0.0), axis=1, keepdims=True)


def row_sum(values):
    return jnp.sum(values, axis=-1, keepdims=True)


def layer_kernel(cfg, names, *refs):
    n_dp, own, count, rows, half, full, hidden, toks, chunks, chunk = cfg
    r = dict(zip(names, refs))
    width = half // 2
    d = lax.axis_index("dp")
    s = lax.axis_index("seq")
    c = s % 2
    x = s // 2
    core = (d, s + 1 - 2 * c)
    across = (d, s + 2 - 4 * x)
    folded = n_dp == 8
    bits = n_dp.bit_length() - 1

    def dp_bit(t):
        return (d // (1 << t)) % 2

    def dp_peer(t):
        m = 1 << t
        return (d + m - 2 * m * dp_bit(t), s)

    a = d // 2
    b = d % 2
    end = a % 3 == 0
    middle = a % 3 != 0
    m = a // 2
    side = dp_peer(0)
    fold = dp_peer(1)
    mirror = ((n_dp // 2 - 1 - a) * 2 + b, s)
    sum_peers = [side, fold, mirror] if folded else [dp_peer(t) for t in range(bits)]

    def remote(src, dst, sems, at, target):
        return pltpu.make_async_remote_copy(
            src_ref=src,
            dst_ref=dst,
            send_sem=r[sems].at[(0,) + at],
            recv_sem=r[sems].at[(1,) + at],
            device_id=target,
            device_id_type=MESH,
        )

    def local(src, dst, sems, at):
        return pltpu.make_async_copy(src, dst, r[sems].at[at])

    win, wout, pin, cin, raw = r["win"], r["wout"], r["pin"], r["cin"], r["raw"]
    ntb, gb, outp, outr, backp, backr = r["ntb"], r["gb"], r["outp"], r["outr"], r["backp"], r["backr"]
    outx, backx, s2o, s2x, s1o, s1x = r["outx"], r["backx"], r["s2o"], r["s2x"], r["s1o"], r["s1x"]
    vown, vother, tg, vg, vec_out = r["vown"], r["vother"], r["tg"], r["vg"], r["vec_out"]
    gbuf, fbuf, mos, gis = r["gbuf"], r["fbuf"], r["mos"], r["gis"]

    mine = pl.multiple_of(x * half, LANE)
    theirs = pl.multiple_of((1 - x) * half, LANE)
    weight_copies = [
        local(r["win_hbm"].at[pl.ds(mine, half)], win.at[pl.ds(0, half)], "sem_w", 0),
        local(r["win_hbm"].at[pl.ds(theirs, half)], win.at[pl.ds(half, half)], "sem_w", 1),
        local(r["wout_hbm"].at[:, pl.ds(mine, half)], wout.at[:, pl.ds(0, half)], "sem_w", 2),
        local(r["wout_hbm"].at[:, pl.ds(theirs, half)], wout.at[:, pl.ds(half, half)], "sem_w", 3),
    ]

    place = pl.ds(pl.multiple_of(c * width, 16), width)

    def p_local(j):
        return local(r["patches"].at[c * own + j], pin.at[j, place], "sem_pl", j)

    def c_local(j):
        return local(r["cot"].at[c * own + j], cin.at[j, place], "sem_cl", j)

    def p_swap(j):
        return remote(r["patches"].at[(1 - c) * own + j], pin.at[j, place], "sem_ps", (j,), core)

    def c_swap(j):
        return remote(r["cot"].at[(1 - c) * own + j], cin.at[j, place], "sem_cs", (j,), core)

    v_swap = remote(r["vmine"], r["vpart"], "sem_v", (0,), core)
    v_across = remote(vown, vother, "sem_v", (1,), across)

    first = pl.ds(0, rows)
    second = pl.ds(rows, rows)
    near = pl.ds(0, half)
    far = pl.ds(half, half)

    def p_across(j):
        return remote(raw.at[j, :, near], raw.at[j, :, far], "sem_px", (j,), across)

    def c_across(j):
        return remote(gb.at[j, first, near], gb.at[j, first, far], "sem_cx", (j,), across)

    def nt_share(j):
        return remote(ntb.at[j, first], ntb.at[j, second], "sem_nt", (j,), core)

    def g_share(j):
        return remote(gb.at[j, first], gb.at[j, second], "sem_g", (j,), core)

    def out_pair(j):
        return remote(outp.at[j, second], outr.at[j], "sem_op", (j,), core)

    def back_pair(j):
        return remote(backp.at[j, second], backr.at[j], "sem_bp", (j,), core)

    def out_across(j):
        return remote(outp.at[j, first, far], outx.at[j], "sem_ox", (j,), across)

    def back_across(j):
        return remote(backp.at[j, first, far], backx.at[j], "sem_bx", (j,), across)

    def s2_across(j):
        return remote(s2o.at[j], s2x.at[j], "sem_s2", (j,), across)

    def s1_across(j):
        return remote(s1o.at[j], s1x.at[j], "sem_s1", (j,), across)

    other = pl.ds(pl.multiple_of((1 - c) * width, 16), width)

    def mixed_give(j):
        return remote(mos.at[j, other], r["mixed"].at[c * own + j], "sem_mg", (j,), core)

    def gin_give(j):
        return remote(gis.at[j, other], r["gin"].at[c * own + j], "sem_gg", (j,), core)

    def mixed_keep(j):
        return local(mos.at[j, place], r["mixed"].at[c * own + j], "sem_mk", j)

    def gin_keep(j):
        return local(gis.at[j, place], r["gin"].at[c * own + j], "sem_gk", j)

    def span(start, size):
        return pl.ds(pl.multiple_of(start, 16), size)

    def add_into(target, at, source, source_at):
        target[at] = (gbuf[at].astype(F32) + r[source][source_at].astype(F32)).astype(BF)


    if folded:
        pairs = chunks // 2
        two, four = chunk // 2, chunk // 4

        def even(k):
            return 2 * k * chunk

        def e_side(k):
            return remote(
                gbuf.at[span(even(k) + (1 - b) * two, two)], r["e0"].at[span(k * two, two)], "sem_e0", (k,), side
            )

        def e_half(k):
            return span(even(k) + b * two, two)

        def e_fold(k):
            return remote(gbuf.at[e_half(k)], r["e1"].at[span(k * two, two)], "sem_e1", (k,), fold)

        def e_mirror(k):
            return remote(
                gbuf.at[span(even(k) + b * two + (1 - m) * four, four)],
                r["e2"].at[span(k * four, four)],
                "sem_e2",
                (k,),
                mirror,
            )

        def e_quarter(k):
            return span(even(k) + b * two + m * four, four)

        def e_mirror_back(k):
            return remote(fbuf.at[e_quarter(k)], fbuf.at[e_quarter(k)], "sem_e3", (k,), mirror)

        def e_fold_back(k):
            return remote(fbuf.at[e_half(k)], fbuf.at[e_half(k)], "sem_e4", (k,), fold)

        def e_side_back(k):
            return remote(fbuf.at[e_half(k)], fbuf.at[e_half(k)], "sem_e5", (k,), side)

        def odd(k):
            return (2 * k + 1) * chunk

        def o_fold(k):
            return remote(gbuf.at[span(odd(k), chunk)], r["o0"].at[span(k * chunk, chunk)], "sem_o0", (k,), fold)

        def o_mirror(k):
            return remote(
                gbuf.at[span(odd(k) + (1 - m) * two, two)], r["o1"].at[span(k * two, two)], "sem_o1", (k,), mirror
            )

        def o_half(k):
            return span(odd(k) + m * two, two)

        def o_rest(k):
            return span(odd(k) + (1 - m) * two, two)

        def o_side(k):
            return remote(
                gbuf.at[span(odd(k) + m * two + (1 - b) * four, four)],
                r["o2"].at[span(k * four, four)],
                "sem_o2",
                (k,),
                side,
            )

        def o_quarter(k):
            return span(odd(k) + m * two + b * four, four)

        def o_side_back(k):
            return remote(fbuf.at[o_quarter(k)], fbuf.at[o_quarter(k)], "sem_o3", (k,), side)

        def o_mirror_back(k):
            return remote(fbuf.at[o_half(k)], fbuf.at[o_half(k)], "sem_o4", (k,), mirror)

        def o_fold_back(k):
            return remote(fbuf.at[o_half(k)], fbuf.at[o_half(k)], "sem_o5", (k,), fold)

        def o_fold_rest(k):
            return remote(fbuf.at[o_rest(k)], fbuf.at[o_rest(k)], "sem_o6", (k,), fold)

        def e_step(e, k):
            if e == 0:
                e_side(k).wait_recv()
                add_into(gbuf, e_half(k), "e0", span(k * two, two))

                @pl.when(end)
                def _():
                    e_fold(k).start()

            elif e == 1:

                @pl.when(middle)
                def _():
                    e_fold(k).wait_recv()
                    add_into(gbuf, e_half(k), "e1", span(k * two, two))
                    e_mirror(k).start()

            elif e == 2:

                @pl.when(middle)
                def _():
                    e_mirror(k).wait_recv()
                    add_into(fbuf, e_quarter(k), "e2", span(k * four, four))
                    e_mirror_back(k).start()

            elif e == 3:

                @pl.when(middle)
                def _():
                    e_mirror_back(k).wait_recv()
                    e_fold_back(k).start()
                    e_side_back(k).start()

            else:

                @pl.when(end)
                def _():
                    e_fold_back(k).wait_recv()
                    e_side_back(k).start()

        def o_step(e, k):
            @pl.when(middle)
            def _():
                if e == 0:
                    o_fold(k).wait_recv()
                    add_into(gbuf, span(odd(k), chunk), "o0", span(k * chunk, chunk))
                    o_mirror(k).start()
                elif e == 1:
                    o_mirror(k).wait_recv()
                    add_into(gbuf, o_half(k), "o1", span(k * two, two))
                    o_side(k).start()
                elif e == 2:
                    o_side(k).wait_recv()
                    add_into(fbuf, o_quarter(k), "o2", span(k * four, four))
                    o_side_back(k).start()
                elif e == 3:
                    o_side_back(k).wait_recv()
                    o_mirror_back(k).start()
                    o_fold_back(k).start()
                else:
                    o_mirror_back(k).wait_recv()
                    o_fold_rest(k).start()

        stages = 5
        ahead = 3

        def o_first(k):
            @pl.when(end)
            def _():
                o_fold(k).start()

        def gradient_first():
            def start(k, carry):
                e_side(k).start()
                return carry

            lax.fori_loop(0, pairs, start, 0)
            for k in range(ahead):
                o_first(k)

        def gradient_step(i):
            @pl.when(i + ahead < pairs)
            def _():
                o_first(i + ahead)

            for e in reversed(range(stages)):
                k = i - e

                @pl.when((k >= 0) & (k < pairs))
                def _(e=e, k=k):
                    e_step(e, k)
                    o_step(e, k)

        def gradient_last(k):
            e_side_back(k).wait_recv()
            e_side(k).wait_send()
            e_side_back(k).wait_send()

            @pl.when(end)
            def _():
                o_fold_back(k).wait_recv()
                o_fold_rest(k).wait_recv()
                e_fold(k).wait_send()
                o_fold(k).wait_send()

            @pl.when(middle)
            def _():
                for make in (e_mirror, e_mirror_back, e_fold_back, o_mirror, o_side, o_side_back):
                    make(k).wait_send()
                for make in (o_mirror_back, o_fold_back, o_fold_rest):
                    make(k).wait_send()

        gradient_ticks = pairs + stages - 1
        gradient_items = pairs
    else:
        def segment(k, t):
            start = k * chunk
            for u in range(t):
                start = start + dp_bit(u) * (chunk >> (u + 1))
            return start

        bases = [chunks * (chunk - (chunk >> t)) for t in range(bits)]

        def rs_at(k, t):
            size = chunk >> (t + 1)
            return span(bases[t] + k * size, size)

        def rs_send(k, t):
            size = chunk >> (t + 1)
            return remote(
                gbuf.at[span(segment(k, t) + (1 - dp_bit(t)) * size, size)],
                r["rbuf"].at[rs_at(k, t)],
                "sem_rs",
                (t, k),
                dp_peer(t),
            )

        def ag_send(k, t):
            at = span(segment(k, t + 1), chunk >> (t + 1))
            return remote(fbuf.at[at], fbuf.at[at], "sem_ag", (t, k), dp_peer(t))

        def gradient_first():
            def start(k, carry):
                rs_send(k, 0).start()
                return carry

            lax.fori_loop(0, chunks, start, 0)

        def gradient_step(i):
            for e in reversed(range(2 * bits - 1)):
                k = i - e

                @pl.when((k >= 0) & (k < chunks))
                def _(e=e, k=k):
                    if e < bits:
                        rs_send(k, e).wait_recv()
                        at = span(segment(k, e + 1), chunk >> (e + 1))
                        add_into(gbuf if e + 1 < bits else fbuf, at, "rbuf", rs_at(k, e))
                        if e + 1 < bits:
                            rs_send(k, e + 1).start()
                        else:
                            ag_send(k, e).start()
                    else:
                        t = 2 * bits - 1 - e
                        ag_send(k, t).wait_recv()
                        ag_send(k, t - 1).start()

        def gradient_last(k):
            ag_send(k, 0).wait_recv()
            for t in range(bits):
                rs_send(k, t).wait_send()
                ag_send(k, t).wait_send()

        gradient_ticks = chunks + 2 * bits - 2
        gradient_items = chunks

    t_half = tg.shape[0] // 2
    t_quarter = t_half // 2
    tc_keep = span(c * t_half, t_half)
    tc_give = span((1 - c) * t_half, t_half)
    tx_keep = span(x * t_quarter, t_quarter)
    tx_give = span((1 - x) * t_quarter, t_quarter)
    t_mine = span(c * t_half + x * t_quarter, t_quarter)
    tb, tcore, tcur, txr, tdp, trd, tall = (r[n] for n in ("tb", "tcore", "tcur", "txr", "tdp", "trd", "tall"))
    vcore, vsend, vrd = r["vcore"], r["vsend"], r["vrd"]
    t_core = remote(tb.at[tc_give], tcore, "sem_t", (0,), core)
    t_across = remote(tcur.at[tx_give], txr, "sem_t", (1,), across)
    t_back_x = remote(tall.at[t_mine], tall.at[t_mine], "sem_t", (2,), across)
    t_back_c = remote(tall.at[tc_keep], tall.at[tc_keep], "sem_t", (3,), core)
    v_core = remote(vg.at[pl.ds(0, 8)], vcore, "sem_t", (4,), core)

    def t_dp(t):
        return remote(tdp.at[t], trd.at[t], "sem_td", (t,), sum_peers[t])

    def v_dp(t):
        return remote(vsend.at[t], vrd.at[t], "sem_vd", (t,), sum_peers[t])

    barrier = pltpu.get_barrier_semaphore()
    peers = [core, across] + sum_peers
    for peer in peers:
        pl.semaphore_signal(barrier, inc=1, device_id=peer, device_id_type=MESH)

    small_names = ("ln1_gain", "ln1_bias", "ln2_gain", "ln2_bias", "chan_out_bias")
    small_names += ("hidden_bias", "tok_in_bias", "tok_out_bias", "tok_in_raw", "tok_out_raw")
    small_copies = [local(r[n], r["in_" + n], "sem_small", at) for at, n in enumerate(small_names)]
    for copy in small_copies:
        copy.start()

    def start_local(j, carry):
        p_local(j).start()
        c_local(j).start()
        return carry

    lax.fori_loop(0, own, start_local, 0)
    for copy in weight_copies:
        copy.start()

    eye, wide = r["eye"], r["wide"]
    eye[...] = jnp.where(diagonal(rows, count), 1.0, 0.0).astype(BF)
    wide[...] = jnp.where(diagonal(half, half), 1.0, 0.0).astype(BF)
    gci, gco, cib = r["gci"], r["gco"], r["cib"]
    gci[...] = jnp.zeros_like(gci)
    gco[...] = jnp.zeros_like(gco)
    cib[...] = jnp.zeros_like(cib)
    tg[...] = jnp.zeros_like(tg)
    vg[...] = jnp.zeros_like(vg)
    s2o[...] = jnp.zeros_like(s2o)
    s1o[...] = jnp.zeros_like(s1o)
    for copy in small_copies:
        copy.wait()
    vpad = r["vpad"]
    vpad[...] = jnp.zeros_like(vpad)
    for at, name in enumerate(small_names[:5]):
        vpad[pl.ds(at, 1), pl.ds(0, width)] = r["in_" + name][...]
    vectors = vpad[...]
    r["vmine"][...] = jnp.where(c == 0, vectors, pltpu.roll(vectors, width, 1))
    hidden_bias = r["hidden_row"]
    for at in range(hidden // LANE):
        hidden_bias[:, pl.ds(at * LANE, LANE)] = r["in_hidden_bias"][pl.ds(at, 1), :]
    for at in range(toks // LANE):
        r["tok_row"][:, pl.ds(at * LANE, LANE)] = r["in_tok_in_bias"][pl.ds(at, 1), :]
    r["tib"][...] = to_column(r["tok_row"][...], toks)
    r["tob"][...] = to_column(r["in_tok_out_bias"][...], rows)
    tok_in_t, tok_in, tok_out, tok_out_t = r["tok_in_t"], r["tok_in"], r["tok_out"], r["tok_out_t"]
    tok_in_t[...] = dot(eye[...], r["in_tok_in_raw"][...]).astype(BF)
    tok_in[...] = dot_nt(wide[...], tok_in_t[...]).astype(BF)
    tok_out[...] = dot(eye[...], r["in_tok_out_raw"][...]).astype(BF)
    tok_out_t[...] = dot_nt(wide[...], tok_out[...]).astype(BF)

    pl.semaphore_wait(barrier, len(peers))

    def start_images(j, carry):
        p_swap(j).start()
        c_swap(j).start()
        return carry

    v_swap.start()
    lax.fori_loop(0, own, start_images, 0)

    def turn_in(ref, j):
        return dot_nt(eye[...], ref[j])

    def turn_out(values):
        return dot_nt(wide[...], values)[:, :count].astype(BF)

    def merge_send(j):
        p_swap(j).wait_recv()
        p_local(j).wait()
        raw[j, :, near] = turn_in(pin, j).astype(BF)
        p_across(j).start()
        c_swap(j).wait_recv()
        c_local(j).wait()
        valid = jnp.where(c * own + j < r["counts"][0], 1.0, 0.0)
        gb[j, first, near] = (turn_in(cin, j) * valid).astype(BF)
        c_across(j).start()

    merge_send(0)
    v_swap.wait_recv()
    vown[...] = r["vmine"][...] + r["vpart"][...]
    v_across.start()
    merge_send(1)
    merge_send(2)

    v_across.wait_recv()

    def vector(row):
        return jnp.concatenate([vown[pl.ds(row, 1), :], vother[pl.ds(row, 1), :]], axis=1)

    def normalise(values):
        centred = values - row_sum(values) * (1.0 / full)
        inverse = lax.rsqrt(row_sum(centred * centred) * (1.0 / full) + EPS)
        return centred * inverse, inverse

    def token_forward(j):
        values = raw[j].astype(F32)
        scaled, inverse = normalise(values)
        normed = (scaled * vector(0) + vector(1)).astype(BF)
        r["sc1"][j] = scaled[:, :half].astype(BF)
        r["inv1"][j] = inverse
        r["n1"][j] = normed[:, :half]
        act, slope = gelu_parts(dot(tok_in[...], normed) + r["tib"][...])
        act = act.astype(BF)
        r["ta"][j] = act[:, :half]
        r["tsl"][j] = slope[:, :half].astype(BF)
        mid = values + (dot(tok_out[...], act) + r["tob"][...])
        r["mid"][j] = mid[:, :half]
        scaled, inverse = normalise(mid)
        r["sc2"][j] = scaled[:, :half].astype(BF)
        r["inv2"][j] = inverse
        ntb[j, first] = (scaled * vector(2) + vector(3)).astype(BF)

    acts, ghs = r["acts"], r["ghs"]

    def channel(j):
        nt = ntb[j]
        g = gb[j]
        step = 256
        for at in range(hidden // step):
            cols = pl.ds(at * step, step)
            pre = dot(nt, win[:, cols]) + hidden_bias[:, cols]
            back = dot_nt(g, wout[cols, :])
            act, slope = gelu_parts(pre)
            acts[:, cols] = act.astype(BF)
            grad = (slope * back).astype(BF)
            ghs[:, cols] = grad
            cib[:, cols] += jnp.sum(grad.astype(F32), axis=0, keepdims=True)
        backp[j] = dot_nt(ghs[...], win[...]).astype(BF)
        back_pair(j).start()
        outp[j] = dot(acts[...], wout[...]).astype(BF)
        out_pair(j).start()
        gco[...] += dot_tn(acts[...], g)
        gci[...] += dot_tn(nt, ghs[...])

    def pair_sums(j):
        back_pair(j).wait_recv()
        total = backp[j, first].astype(F32) + backr[j].astype(F32)
        s2o[j, pl.ds(0, 1)] = to_row(row_sum(total * vector(2)), rows)
        s2o[j, pl.ds(1, 1)] = to_row(row_sum(total * (ntb[j, first].astype(F32) - vector(3))), rows)
        backp[j, first] = total.astype(BF)
        s2_across(j).start()
        back_across(j).start()

    def gather_phase(j, carry):
        @pl.when(j + 3 < own)
        def _():
            merge_send(j + 3)

        @pl.when(j < own)
        def _():
            p_across(j).wait_recv()
            token_forward(j)
            nt_share(j).start()
            c_across(j).wait_recv()
            g_share(j).start()

        @pl.when(j == 0)
        def _():
            for copy in weight_copies:
                copy.wait()

        @pl.when(j > 0)
        def _():
            nt_share(j - 1).wait_recv()
            g_share(j - 1).wait_recv()
            channel(j - 1)

        @pl.when(j > 1)
        def _():
            pair_sums(j - 2)

        return carry

    lax.fori_loop(0, own + 1, gather_phase, 0)

    tiles = hidden // LANE
    for at in range(tiles):
        gbuf[pl.ds(at * full, full)] = gci[:, pl.ds(at * LANE, LANE)].astype(BF)
    for at in range(full // LANE):
        gbuf[pl.ds(tiles * full + at * hidden, hidden)] = gco[:, pl.ds(at * LANE, LANE)].astype(BF)
    gradient_first()
    pair_sums(own - 1)

    def pair_outs(j):
        out_pair(j).wait_recv()
        total = outp[j, first].astype(F32) + outr[j].astype(F32)
        outp[j, first] = total.astype(BF)
        out_across(j).start()

    def norm_back(weighted, scaled, inverse, sums):
        mean = to_column(sums[0:1] * (1.0 / full), rows)
        slant = to_column(sums[1:2] * (1.0 / full), rows)
        return inverse * (weighted - mean - scaled * slant)

    def token_backward(j):
        s2_across(j).wait_recv()
        back_across(j).wait_recv()
        grad_normed = backp[j, first, near].astype(F32) + backx[j].astype(F32)
        scaled = r["sc2"][j].astype(F32)
        grad_out = gb[j, first, near].astype(F32)
        weighted = grad_normed * vown[pl.ds(2, 1), :]
        grad_mid = grad_out + norm_back(weighted, scaled, r["inv2"][j], s2o[j] + s2x[j])
        r["gm"][j] = grad_mid
        vg[pl.ds(2, 1), :] += jnp.sum(grad_normed * scaled, axis=0, keepdims=True)
        vg[pl.ds(3, 1), :] += jnp.sum(grad_normed, axis=0, keepdims=True)
        vg[pl.ds(4, 1), :] += jnp.sum(grad_out, axis=0, keepdims=True)
        low = grad_mid.astype(BF)
        ones = jnp.ones((8, half), BF)
        tg[pl.ds(rows, rows), :] += dot_nt(low, r["ta"][j])
        tg[pl.ds(2 * rows + 8, 8), pl.ds(0, rows)] += dot_nt(ones, low)
        grad_pre = (r["tsl"][j].astype(F32) * dot(tok_out_t[...], low)).astype(BF)
        tg[pl.ds(0, rows), :] += dot_nt(r["n1"][j], grad_pre)
        tg[pl.ds(2 * rows, 8), :] += dot_nt(ones, grad_pre)
        grad_one = dot(tok_in_t[...], grad_pre)
        scaled = r["sc1"][j].astype(F32)
        vg[pl.ds(0, 1), :] += jnp.sum(grad_one * scaled, axis=0, keepdims=True)
        vg[pl.ds(1, 1), :] += jnp.sum(grad_one, axis=0, keepdims=True)
        weighted = grad_one * vown[pl.ds(0, 1), :]
        r["w1"][j] = weighted
        s1o[j, pl.ds(0, 1)] = to_row(row_sum(weighted), rows)
        s1o[j, pl.ds(1, 1)] = to_row(row_sum(weighted * scaled), rows)
        s1_across(j).start()

    def input_grad(j):
        s1_across(j).wait_recv()
        scaled = r["sc1"][j].astype(F32)
        grad = r["gm"][j] + norm_back(r["w1"][j], scaled, r["inv1"][j], s1o[j] + s1x[j])
        gis[j] = turn_out(grad.astype(BF))
        gin_give(j).start()
        gin_keep(j).start()

    def mixed_part(j):
        out_across(j).wait_recv()
        total = outp[j, first, near].astype(F32) + outx[j].astype(F32)
        valid = jnp.where(c * own + j < r["counts"][0], 1.0, 0.0)
        mos[j] = turn_out((valid * (r["mid"][j] + (total + vown[pl.ds(4, 1), :]))).astype(BF))
        mixed_give(j).start()
        mixed_keep(j).start()

    def token_step(e):
        if e == 0:
            tb[...] = tg[...].astype(BF)
            for at in range(hidden // half):
                vg[pl.ds(8 + at, 1), :] = cib[:, pl.ds(at * half, half)]
            t_core.start()
            v_core.start()
        elif e == 1:
            t_core.wait_recv()
            v_core.wait_recv()
            tcur[...] = (tb[tc_keep].astype(F32) + tcore[...].astype(F32)).astype(BF)
            t_across.start()
            vsend[0, pl.ds(0, 8)] = vg[pl.ds(0, 8)] + vcore[...]
            vsend[0, pl.ds(8, 8)] = vg[pl.ds(8, 8)]
            v_dp(0).start()
        elif e == 2:
            t_across.wait_recv()
            tdp[0] = (tcur[tx_keep].astype(F32) + txr[...].astype(F32)).astype(BF)
            t_dp(0).start()
        elif e < 3 + bits:
            t = e - 3
            t_dp(t).wait_recv()
            v_dp(t).wait_recv()
            total = (tdp[t].astype(F32) + trd[t].astype(F32)).astype(BF)
            vec = vsend[t] + vrd[t]
            if t + 1 < bits:
                tdp[t + 1] = total
                vsend[t + 1] = vec
                t_dp(t + 1).start()
                v_dp(t + 1).start()
            else:
                tall[t_mine] = total
                t_back_x.start()
                vec_out[pl.ds(0, 8), :] = jnp.where(c == 0, vec, pltpu.roll(vec, width, 1))[:8]
                vec_out[pl.ds(8, 8), :] = vec[8:]
        elif e == 3 + bits:
            t_back_x.wait_recv()
            t_back_c.start()
        else:
            t_back_c.wait_recv()
            vec_out[pl.ds(16, 16), :] = tall[pl.ds(2 * rows, 16)].astype(F32)

    token_first = own
    token_steps = 5 + bits
    outs_first = own // 2
    mixed_first = 2 * own - 1

    def scatter_phase(i, carry):
        gradient_step(i)

        @pl.when(i < own)
        def _():
            token_backward(i)

        for e in range(token_steps):

            @pl.when(i == token_first + e)
            def _(e=e):
                token_step(e)

        @pl.when((i > 0) & (i <= own))
        def _():
            input_grad(i - 1)

        @pl.when((i >= outs_first) & (i < outs_first + own))
        def _():
            pair_outs(i - outs_first)

        @pl.when((i >= mixed_first) & (i < mixed_first + own))
        def _():
            mixed_part(i - mixed_first)

        return carry

    lax.fori_loop(0, max(gradient_ticks, token_first + token_steps, mixed_first + own), scatter_phase, 0)

    def gradient_end(k, carry):
        gradient_last(k)
        return carry

    lax.fori_loop(0, gradient_items, gradient_end, 0)

    outs = []
    for at in range(tiles):
        lanes = pl.ds(at * LANE, LANE)
        for part, to in enumerate((mine, theirs)):
            outs.append((fbuf.at[pl.ds(at * full + part * half, half)], r["g_chan_in"].at[pl.ds(to, half), lanes]))
    for at in range(full // LANE):
        to = mine if at < half // LANE else theirs
        lanes = pl.ds(pl.multiple_of(to + (at % (half // LANE)) * LANE, LANE), LANE)
        outs.append((fbuf.at[pl.ds(tiles * full + at * hidden, hidden)], r["g_chan_out"].at[:, lanes]))
    outs = [local(src, dst, "sem_out", at) for at, (src, dst) in enumerate(outs)]
    for copy in outs:
        copy.start()

    def drain(j, carry):
        for make in (p_swap, c_swap, p_across, c_across, nt_share, g_share, out_pair, back_pair):
            make(j).wait_send()
        for make in (out_across, back_across, s2_across, s1_across):
            make(j).wait_send()
        for make in (mixed_give, gin_give, mixed_keep, gin_keep):
            make(j).wait()
        return carry

    lax.fori_loop(0, own, drain, 0)
    for copy in [v_swap, v_across, t_core, t_across, t_back_x, t_back_c, v_core]:
        copy.wait_send()
    for t in range(bits):
        t_dp(t).wait_send()
        v_dp(t).wait_send()
    for copy in outs:
        copy.wait()


def run_layer(n_dp, **arrays):
    batch, width, count = arrays["patches"].shape
    own = batch // 2
    full, hidden = arrays["win_hbm"].shape
    half = full // 2
    toks = arrays["tok_in_raw"].shape[1]
    rows = -(-count // 16) * 16
    bits = n_dp.bit_length() - 1
    grad_rows = 2 * full * hidden // LANE
    folded = n_dp == 8
    choices = (24, 12, 6, 2) if folded else (9, 3, 1)
    parts = 4 if folded else n_dp
    chunks = next(k for k in choices if grad_rows % (k * parts * 16) == 0)
    chunk = grad_rows // chunks
    cfg = (n_dp, own, count, rows, half, full, hidden, toks, chunks, chunk)
    vmem = pltpu.VMEM
    dma = pltpu.SemaphoreType.DMA
    pairs = chunks // 2
    two, four = chunk // 2, chunk // 4
    t_rows = -(-(2 * rows + 16) // 64) * 64
    scratch = {
        "win": vmem((full, hidden), BF),
        "wout": vmem((hidden, full), BF),
        "pin": vmem((own, half, count), BF),
        "cin": vmem((own, half, count), BF),
        "vpad": vmem((8, half), F32),
        "hidden_row": vmem((1, hidden), F32),
        "tok_row": vmem((1, toks), F32),
        "vmine": vmem((8, half), F32),
        "vpart": vmem((8, half), F32),
        "vown": vmem((8, half), F32),
        "vother": vmem((8, half), F32),
        "eye": vmem((rows, count), BF),
        "wide": vmem((half, half), BF),
        "tok_in_t": vmem((rows, toks), BF),
        "tok_in": vmem((toks, rows), BF),
        "tok_out": vmem((rows, toks), BF),
        "tok_out_t": vmem((toks, rows), BF),
        "tib": vmem((toks, 1), F32),
        "tob": vmem((rows, 1), F32),
        "raw": vmem((own, rows, full), BF),
        "ntb": vmem((own, 2 * rows, full), BF),
        "gb": vmem((own, 2 * rows, full), BF),
        "acts": vmem((2 * rows, hidden), BF),
        "ghs": vmem((2 * rows, hidden), BF),
        "gci": vmem((full, hidden), F32),
        "gco": vmem((hidden, full), F32),
        "cib": vmem((1, hidden), F32),
        "outp": vmem((own, 2 * rows, full), BF),
        "outr": vmem((own, rows, full), BF),
        "backp": vmem((own, 2 * rows, full), BF),
        "backr": vmem((own, rows, full), BF),
        "outx": vmem((own, rows, half), BF),
        "backx": vmem((own, rows, half), BF),
        "s2o": vmem((own, 8, rows), F32),
        "s2x": vmem((own, 8, rows), F32),
        "s1o": vmem((own, 8, rows), F32),
        "s1x": vmem((own, 8, rows), F32),
        "n1": vmem((own, rows, half), BF),
        "ta": vmem((own, toks, half), BF),
        "tsl": vmem((own, toks, half), BF),
        "mid": vmem((own, rows, half), F32),
        "sc1": vmem((own, rows, half), BF),
        "sc2": vmem((own, rows, half), BF),
        "inv1": vmem((own, rows, 1), F32),
        "inv2": vmem((own, rows, 1), F32),
        "gm": vmem((own, rows, half), F32),
        "w1": vmem((own, rows, half), F32),
        "gis": vmem((own, half, count), BF),
        "mos": vmem((own, half, count), BF),
        "gbuf": vmem((grad_rows, LANE), BF),
        "fbuf": vmem((grad_rows, LANE), BF),
        "tg": vmem((t_rows, toks), F32),
        "tb": vmem((t_rows, toks), BF),
        "tcore": vmem((t_rows // 2, toks), BF),
        "tcur": vmem((t_rows // 2, toks), BF),
        "txr": vmem((t_rows // 4, toks), BF),
        "tdp": vmem((bits, t_rows // 4, toks), BF),
        "trd": vmem((bits, t_rows // 4, toks), BF),
        "vg": vmem((16, half), F32),
        "vcore": vmem((8, half), F32),
        "vsend": vmem((bits, 16, half), F32),
        "vrd": vmem((bits, 16, half), F32),
        "sem_w": dma((4,)),
        "sem_small": dma((10,)),
        "sem_v": dma((2, 2)),
        "sem_out": dma((2 * (hidden // LANE) + full // LANE,)),
        "sem_t": dma((2, 5)),
        "sem_td": dma((2, bits)),
        "sem_vd": dma((2, bits)),
    }
    for name in arrays:
        if name not in ("counts", "patches", "cot", "win_hbm", "wout_hbm"):
            scratch["in_" + name] = vmem(arrays[name].shape, arrays[name].dtype)
    for name in ("pl", "cl", "mk", "gk"):
        scratch["sem_" + name] = dma((own,))
    for name in ("ps", "cs", "px", "cx", "nt", "g", "op", "bp", "ox", "bx", "s2", "s1", "mg", "gg"):
        scratch["sem_" + name] = dma((2, own))
    if folded:
        scratch["e0"] = vmem((pairs * two, LANE), BF)
        scratch["e1"] = vmem((pairs * two, LANE), BF)
        scratch["e2"] = vmem((pairs * four, LANE), BF)
        scratch["o0"] = vmem((pairs * chunk, LANE), BF)
        scratch["o1"] = vmem((pairs * two, LANE), BF)
        scratch["o2"] = vmem((pairs * four, LANE), BF)
        for name in ("e0", "e1", "e2", "e3", "e4", "e5", "o0", "o1", "o2", "o3", "o4", "o5", "o6"):
            scratch["sem_" + name] = dma((2, pairs))
    else:
        scratch["rbuf"] = vmem((chunks * (chunk - (chunk >> bits)), LANE), BF)
        scratch["sem_rs"] = dma((2, bits, chunks))
        scratch["sem_ag"] = dma((2, bits, chunks))
    hbm = pl.BlockSpec(memory_space=pl.ANY)
    inside = pl.BlockSpec(memory_space=pltpu.VMEM)
    places = {"counts": pl.BlockSpec(memory_space=pltpu.SMEM), "tall": inside, "vec_out": inside}
    outs = {
        "mixed": ((batch, width, count), BF),
        "gin": ((batch, width, count), BF),
        "tall": ((t_rows, toks), BF),
        "vec_out": ((32, half), F32),
        "g_chan_in": ((full, hidden), BF),
        "g_chan_out": ((hidden, full), BF),
    }
    names = list(arrays) + list(outs) + list(scratch)
    results = pl.pallas_call(
        functools.partial(layer_kernel, cfg, names),
        out_shape=tuple(jax.ShapeDtypeStruct(*outs[name]) for name in outs),
        in_specs=[places.get(name, hbm) for name in arrays],
        out_specs=tuple(places.get(name, hbm) for name in outs),
        scratch_shapes=list(scratch.values()),
        compiler_params=pltpu.CompilerParams(
            collective_id=0, has_side_effects=True, vmem_limit_bytes=63 * 2**20
        ),
        name="mixer_layer",
    )(*arrays.values())
    return dict(zip(outs, results))


def finish_kernel(names, *refs):
    r = dict(zip(names, refs))
    sems = r["sems"]
    count, toks = r["tok_in"].shape
    rows = -(-count // 16) * 16
    parts = r["pieces"].shape[1]
    step = r["pieces"].shape[2]
    loads, stores = [], []
    whole_in, whole_out = [], []
    for at, name in enumerate(("mixed", "gin")):
        for part in range(2):
            here = pl.ds(part * (r["images"].shape[1] // 2), r["images"].shape[1] // 2)
            sem = 2 + 4 * parts + 4 * at + 2 * part
            whole_in.append(pltpu.make_async_copy(r[name + "_raw"].at[here], r["images"].at[at, here], sems.at[sem]))
            whole_out.append(pltpu.make_async_copy(r["images"].at[at, here], r[name].at[here], sems.at[sem + 1]))
    for at, name in enumerate(("chan_in", "chan_out")):
        for part in range(parts):
            here = pl.ds(part * step, step)
            sem = 2 + at * parts + part
            loads.append(pltpu.make_async_copy(r[name + "_raw"].at[here], r["pieces"].at[at, part], sems.at[sem]))
            stores.append(
                pltpu.make_async_copy(r["wide"].at[at, part], r[name].at[here], sems.at[sem + 2 * parts])
            )
    for copy in loads + whole_in:
        copy.start()
    for at in range(len(loads)):
        loads[at].wait()
        r["wide"][at // parts, at % parts] = r["pieces"][at // parts, at % parts].astype(F32)
        stores[at].start()
    for at in range(len(whole_in)):
        whole_in[at].wait()
        whole_out[at].start()
    vec, tall = r["vec_raw"], r["tok_raw"]
    width = r["ln1_gain"].shape[1]
    for at, name in enumerate(("ln1_gain", "ln1_bias", "ln2_gain", "ln2_bias", "chan_out_bias")):
        r[name][...] = vec[pl.ds(at, 1), :][:, :width]
    half = vec.shape[1]
    for at in range(r["chan_in_bias"].shape[0]):
        row, lane = divmod(at * LANE, half)
        r["chan_in_bias"][pl.ds(at, 1), :] = vec[pl.ds(8 + row, 1), pl.ds(lane, LANE)]
    for at in range(toks // LANE):
        r["tok_in_bias"][pl.ds(at, 1), :] = vec[pl.ds(16, 1), pl.ds(at * LANE, LANE)]
    r["tok_out_bias"][...] = vec[pl.ds(24, 1), :][:, :count]
    r["tok_in"][...] = tall[pl.ds(0, rows)][:count].astype(F32)
    r["tok_out"][...] = tall[pl.ds(rows, rows)][:count].astype(F32)
    for copy in stores + whole_out:
        copy.wait()


def finish(out, count, width):
    full, hidden = out["g_chan_in"].shape
    toks = out["tall"].shape[1]
    hbm = pl.BlockSpec(memory_space=pl.ANY)
    inside = pl.BlockSpec(memory_space=pltpu.VMEM)
    arrays = {
        "mixed_raw": out["mixed"],
        "gin_raw": out["gin"],
        "chan_in_raw": out["g_chan_in"],
        "chan_out_raw": out["g_chan_out"],
        "tok_raw": out["tall"],
        "vec_raw": out["vec_out"],
    }
    outs = {
        "mixed": (out["mixed"].shape, BF),
        "gin": (out["gin"].shape, BF),
        "chan_in": ((full, hidden), F32),
        "chan_out": ((hidden, full), F32),
        "ln1_gain": ((1, width), F32),
        "ln1_bias": ((1, width), F32),
        "ln2_gain": ((1, width), F32),
        "ln2_bias": ((1, width), F32),
        "chan_out_bias": ((1, width), F32),
        "chan_in_bias": ((hidden // LANE, LANE), F32),
        "tok_in_bias": ((toks // LANE, LANE), F32),
        "tok_out_bias": ((1, count), F32),
        "tok_in": ((count, toks), F32),
        "tok_out": ((count, toks), F32),
    }
    parts = 4
    scratch = {
        "pieces": pltpu.VMEM((2, parts, full // parts, hidden), BF),
        "wide": pltpu.VMEM((2, parts, full // parts, hidden), F32),
        "images": pltpu.VMEM((2,) + out["mixed"].shape, BF),
        "sems": pltpu.SemaphoreType.DMA((10 + 4 * parts,)),
    }
    names = list(arrays) + list(outs) + list(scratch)
    results = pl.pallas_call(
        functools.partial(finish_kernel, names),
        out_shape=tuple(jax.ShapeDtypeStruct(*outs[name]) for name in outs),
        in_specs=[hbm] * 4 + [inside] * 2,
        out_specs=(hbm,) * 4 + (inside,) * 10,
        scratch_shapes=list(scratch.values()),
        compiler_params=pltpu.CompilerParams(vmem_limit_bytes=63 * 2**20),
        name="finish",
    )(*arrays.values())
    return dict(zip(outs, results))


def per_device(
    n_dp,
    image_counts,
    patches,
    ln1_gain,
    ln1_bias,
    tok_in_weight,
    tok_in_bias,
    tok_out_weight,
    tok_out_bias,
    ln2_gain,
    ln2_bias,
    chan_in_weight,
    chan_in_bias,
    chan_out_weight,
    chan_out_bias,
    cotangent,
):
    out = run_layer(
        n_dp,
        counts=image_counts,
        patches=jnp.transpose(patches, (1, 2, 0)),
        cot=jnp.transpose(cotangent, (1, 2, 0)),
        ln1_gain=ln1_gain[None, :],
        ln1_bias=ln1_bias[None, :],
        ln2_gain=ln2_gain[None, :],
        ln2_bias=ln2_bias[None, :],
        chan_out_bias=chan_out_bias[None, :],
        hidden_bias=chan_in_bias.reshape(-1, LANE),
        tok_in_bias=tok_in_bias.reshape(-1, LANE),
        tok_out_bias=tok_out_bias[None, :],
        tok_in_raw=tok_in_weight.T,
        tok_out_raw=tok_out_weight,
        win_hbm=chan_in_weight,
        wout_hbm=chan_out_weight,
    )
    out = finish(out, patches.shape[0], patches.shape[2])
    return (
        jnp.transpose(out["mixed"], (2, 0, 1)),
        jnp.transpose(out["gin"], (2, 0, 1)),
        out["ln1_gain"][0],
        out["ln1_bias"][0],
        out["tok_in"].T,
        out["tok_in_bias"].reshape(-1),
        out["tok_out"],
        out["tok_out_bias"][0],
        out["ln2_gain"][0],
        out["ln2_bias"][0],
        out["chan_in"],
        out["chan_in_bias"].reshape(-1),
        out["chan_out"],
        out["chan_out_bias"][0],
    )


def solution(mesh):
    in_specs = (
        P("dp"),
        P(None, "dp", "seq"),
        P("seq"),
        P("seq"),
        P(),
        P(),
        P(),
        P(),
        P("seq"),
        P("seq"),
        P(None, "seq"),
        P("seq"),
        P("seq", None),
        P("seq"),
        P(None, "dp", "seq"),
    )
    out_specs = (
        P(None, "dp", "seq"),
        P(None, "dp", "seq"),
        P("seq"),
        P("seq"),
        P(),
        P(),
        P(),
        P(),
        P("seq"),
        P("seq"),
        P(None, "seq"),
        P("seq"),
        P("seq", None),
        P("seq"),
    )
    return jax.shard_map(
        functools.partial(per_device, mesh.shape["dp"]),
        mesh=mesh,
        in_specs=in_specs,
        out_specs=out_specs,
        check_vma=False,
    )
```

time: 590 us -> 144 us (0.24); the launches traced: 584 us -> 144 us
  waiting for transfers between devices: 321 us -> 0 us
  Pallas kernels: 0 us -> 142 us
  blocking collectives: 136 us -> 0 us
  matrix products: 70.8 us -> 0 us
  other arithmetic: 27.6 us -> 0 us
  between operations: 15.5 us -> 1.3 us
  local copies, waits for them, and re-layouts: 12.3 us -> 0 us
    psum x2 -> x0, waiting for transfers between devices: 206 us -> none  [the longest x1 133 us: per_device(): lax.psum((grad_tok_in, grad_tok_in_bias, grad_tok_out, grad_tok_out_bias)...]
    pallas_call x0 -> x2, Pallas kernels: none -> 142 us  [the longest x1 136 us: run_layer(): pl.pallas_call(functools.partial(layer_kernel, cfg, names), out_shape=tup...]
    psum x8 -> x0, blocking collectives: 136 us -> none  [the longest x4 44.8 us: feature_sum(): return lax.psum(jnp.sum(values, axis=-1, keepdims=True), 'seq')]
    dot_general x12 -> x0, matrix products: 70.8 us -> none  [the longest x1 12.5 us: per_device(): jnp.einsum('pbh,pbc->hc', hidden_act, all_grad, preferred_element_type=jn...]
    all_gather x2 -> x0, waiting for transfers between devices: 64.7 us -> none  [the longest x1 33.8 us: per_device(): all_normed_two = lax.all_gather(normed_two, 'seq', axis=2, tiled=True)]
    reduce_scatter x2 -> x0, waiting for transfers between devices: 50.3 us -> none  [the longest x1 33.8 us: per_device(): lax.psum_scatter(partial_out.astype(jnp.bfloat16), 'seq', scatter_dimensi...]
    reduce_sum x6 -> x0, other arithmetic: 13.6 us -> none  [the longest x1 5.08 us: per_device(): grad_tok_out_bias = jnp.sum(grad_token_out, axis=(1, 2), dtype=jnp.float32)]
    unnamed x70 -> x0, local copies, waits for them, and re-layouts: 12.3 us -> none
  transfers between devices with their start and end apart: 6 -> 0, of which waited for: 6 -> 0; matrix products, arithmetic and copies ran while one was open for 12% -> 0% of each run, Pallas kernels for 0% -> 0%
where the time goes in v2:
time: 144 us
  Pallas kernels  142 us (99%)
    pallas_call x1, Pallas kernels, run_layer(): pl.pallas_call(functools.partial(layer_kernel, cfg, names), out_shape=tup...  136 us
    pallas_call x1, Pallas kernels, finish(): pl.pallas_call(functools.partial(finish_kernel, names), out_shape=tuple((...  6.19 us

profile of v2, /device:TPU:0, one launch (start us, length us, event | category | flops | bytes accessed | tf_op | source)
XLA Modules:
  0.0 143.7 jit_solution(12410595311602600257)
XLA Ops:
  1.3 136.2 %mixer_layer.1 = (bf16[12,192,196]{2,1,0:T(8,128)(2,1)}, bf16[12,192,196]{2,1,0:T(8,128)(2,1)}, bf16[448,384]{1,0:T(8,128)(2,1)}, f32[32,384]{1,0:T(8,128)}, bf1...) custom-call(s32[1]{0:T(128)S(6)} %copy.29.refs_0_, bf16[12,192,196]{2,1,0:T(8,128)(2,1)} %bitcast.22, ...), custom_call_target="tpu_custom_call" | custom-call | tf_op jit(solution)/shard_map/mixer_layer/pallas_call | solution.py:943
  137.5 6.2 %finish.1 = (bf16[12,192,196]{2,1,0:T(8,128)(2,1)}, bf16[12,192,196]{2,1,0:T(8,128)(2,1)}, f32[768,768]{1,0:T(8,128)}, f32[768,768]{1,0:T(8,128)}, f32[1,192]{1,...) custom-call(bf16[12,192,196]{2,1,0:T(8,128)(2,1)} %get-tuple-element, ...), custom_call_target="tpu_custom_call" | custom-call | tf_op jit(solution)/shard_map/finish/pallas_call | solution.py:1043

commit v3 on v2

v3 whole, which is shorter than its diff:
```python
import functools
from types import SimpleNamespace

import jax
import jax.numpy as jnp
from jax import lax
from jax.experimental import pallas as pl
from jax.experimental.pallas import tpu as pltpu
from jax.sharding import PartitionSpec as P

MESH = pl.DeviceIdType.MESH
BF = jnp.bfloat16
F32 = jnp.float32
EPS = 1e-06
GELU_A = 0.7978845608028654
GELU_B = GELU_A * 0.044715
LANE = 128


def gelu_parts(x):
    square = x * x
    tanh = jnp.tanh(x * (GELU_A + GELU_B * square))
    half = 0.5 + 0.5 * tanh
    slope = half + (0.5 * x) * (1.0 - tanh * tanh) * (GELU_A + (3.0 * GELU_B) * square)
    return x * half, slope


def gelu(x):
    return x * (0.5 + 0.5 * jnp.tanh(x * (GELU_A + GELU_B * (x * x))))


def dot(a, b):
    return lax.dot_general(a, b, (((1,), (0,)), ((), ())), preferred_element_type=F32)


def dot_nt(a, b):
    return lax.dot_general(a, b, (((1,), (1,)), ((), ())), preferred_element_type=F32)


def dot_tn(a, b):
    return lax.dot_general(a, b, (((0,), (0,)), ((), ())), preferred_element_type=F32)


def diagonal(rows, columns):
    return lax.broadcasted_iota(jnp.int32, (rows, columns), 0) == lax.broadcasted_iota(
        jnp.int32, (rows, columns), 1
    )


def to_row(values, columns):
    return jnp.sum(jnp.where(diagonal(values.shape[0], columns), values, 0.0), axis=0, keepdims=True)


def to_column(values, rows):
    return jnp.sum(jnp.where(diagonal(rows, values.shape[1]), values, 0.0), axis=1, keepdims=True)


def row_sum(values):
    return jnp.sum(values, axis=-1, keepdims=True)


def layer_kernel(cfg, names, *refs):
    n_dp, own, count, rows, half, full, hidden, toks, chunks, chunk = cfg
    r = SimpleNamespace(**dict(zip(names, refs)))
    width = half // 2
    d = lax.axis_index("dp")
    s = lax.axis_index("seq")
    c = s % 2
    x = s // 2
    core = (d, s + 1 - 2 * c)
    across = (d, s + 2 - 4 * x)
    folded = n_dp == 8
    bits = n_dp.bit_length() - 1

    def dp_bit(t):
        return (d // (1 << t)) % 2

    def dp_peer(t):
        m = 1 << t
        return (d + m - 2 * m * dp_bit(t), s)

    a = d // 2
    b = d % 2
    end = a % 3 == 0
    middle = a % 3 != 0
    m = a // 2
    side = dp_peer(0)
    fold = dp_peer(1)
    mirror = ((n_dp // 2 - 1 - a) * 2 + b, s)
    sum_peers = [side, fold, mirror] if folded else [dp_peer(t) for t in range(bits)]

    def remote(src, dst, sems, at, target):
        return pltpu.make_async_remote_copy(
            src_ref=src,
            dst_ref=dst,
            send_sem=sems.at[(0,) + at],
            recv_sem=sems.at[(1,) + at],
            device_id=target,
            device_id_type=MESH,
        )

    def local(src, dst, sems, at):
        return pltpu.make_async_copy(src, dst, sems.at[at])

    win, wout, pin, cin, raw = r.win, r.wout, r.pin, r.cin, r.raw
    ntb, gb, outp, outr, backp, backr = r.ntb, r.gb, r.outp, r.outr, r.backp, r.backr
    outx, backx, s2o, s2x, s1o, s1x = r.outx, r.backx, r.s2o, r.s2x, r.s1o, r.s1x
    vown, vother, tg, vg, vec_out = r.vown, r.vother, r.tg, r.vg, r.vec_out
    gbuf, fbuf = r.gbuf, r.fbuf
    mos, gis = pin, cin

    mine = pl.multiple_of(x * half, LANE)
    theirs = pl.multiple_of((1 - x) * half, LANE)
    weight_copies = [
        local(r.win_hbm.at[pl.ds(mine, half)], win.at[pl.ds(0, half)], r.sem_w, 0),
        local(r.win_hbm.at[pl.ds(theirs, half)], win.at[pl.ds(half, half)], r.sem_w, 1),
        local(r.wout_hbm.at[:, pl.ds(mine, half)], wout.at[:, pl.ds(0, half)], r.sem_w, 2),
        local(r.wout_hbm.at[:, pl.ds(theirs, half)], wout.at[:, pl.ds(half, half)], r.sem_w, 3),
    ]

    place = pl.ds(pl.multiple_of(c * width, 16), width)

    def p_local(j):
        return local(r.patches.at[c * own + j], pin.at[j, place], r.sem_pl, j)

    def c_local(j):
        return local(r.cot.at[c * own + j], cin.at[j, place], r.sem_cl, j)

    def p_swap(j):
        return remote(r.patches.at[(1 - c) * own + j], pin.at[j, place], r.sem_ps, (j,), core)

    def c_swap(j):
        return remote(r.cot.at[(1 - c) * own + j], cin.at[j, place], r.sem_cs, (j,), core)

    v_swap = remote(r.vmine, r.vpart, r.sem_v, (0,), core)
    v_across = remote(vown, vother, r.sem_v, (1,), across)

    first = pl.ds(0, rows)
    second = pl.ds(rows, rows)
    near = pl.ds(0, half)
    far = pl.ds(half, half)

    def p_across(j):
        return remote(raw.at[j, :, near], raw.at[j, :, far], r.sem_px, (j,), across)

    def c_across(j):
        return remote(gb.at[j, first, near], gb.at[j, first, far], r.sem_cx, (j,), across)

    def nt_share(j):
        return remote(ntb.at[j, first], ntb.at[j, second], r.sem_nt, (j,), core)

    def g_share(j):
        return remote(gb.at[j, first], gb.at[j, second], r.sem_g, (j,), core)

    def out_pair(j):
        return remote(outp.at[j, second], outr.at[j], r.sem_op, (j,), core)

    def back_pair(j):
        return remote(backp.at[j, second], backr.at[j], r.sem_bp, (j,), core)

    def out_across(j):
        return remote(outp.at[j, first, far], outx.at[j], r.sem_ox, (j,), across)

    def back_across(j):
        return remote(backp.at[j, first, far], backx.at[j], r.sem_bx, (j,), across)

    def s2_across(j):
        return remote(s2o.at[j], s2x.at[j], r.sem_s2, (j,), across)

    def s1_across(j):
        return remote(s1o.at[j], s1x.at[j], r.sem_s1, (j,), across)

    other = pl.ds(pl.multiple_of((1 - c) * width, 16), width)

    def mixed_give(j):
        return remote(mos.at[j, other], r.mixed.at[c * own + j], r.sem_mg, (j,), core)

    def gin_give(j):
        return remote(gis.at[j, other], r.gin.at[c * own + j], r.sem_gg, (j,), core)

    def mixed_keep(j):
        return local(mos.at[j, place], r.mixed.at[c * own + j], r.sem_mk, j)

    def gin_keep(j):
        return local(gis.at[j, place], r.gin.at[c * own + j], r.sem_gk, j)

    def span(start, size):
        return pl.ds(pl.multiple_of(start, 16), size)

    def add_into(target, at, source, source_at):
        target[at] = (gbuf[at].astype(F32) + source[source_at].astype(F32)).astype(BF)


    if folded:
        pairs = chunks
        two, four = chunk * 13 // 36, chunk * 13 // 72

        def even(k):
            return k * chunk

        def e_side(k):
            return remote(
                gbuf.at[span(even(k) + (1 - b) * two, two)], r.e0.at[span(k * two, two)], r.sem_e0, (k,), side
            )

        def e_half(k):
            return span(even(k) + b * two, two)

        def e_fold(k):
            return remote(gbuf.at[e_half(k)], r.e1.at[span(k * two, two)], r.sem_e1, (k,), fold)

        def e_mirror(k):
            return remote(
                gbuf.at[span(even(k) + b * two + (1 - m) * four, four)],
                r.e2.at[span(k * four, four)],
                r.sem_e2,
                (k,),
                mirror,
            )

        def e_quarter(k):
            return span(even(k) + b * two + m * four, four)

        def e_mirror_back(k):
            return remote(fbuf.at[e_quarter(k)], fbuf.at[e_quarter(k)], r.sem_e3, (k,), mirror)

        def e_fold_back(k):
            return remote(fbuf.at[e_half(k)], fbuf.at[e_half(k)], r.sem_e4, (k,), fold)

        def e_side_back(k):
            return remote(fbuf.at[e_half(k)], fbuf.at[e_half(k)], r.sem_e5, (k,), side)

        whole, three, six = chunk * 5 // 18, chunk * 5 // 36, chunk * 5 // 72

        def odd(k):
            return k * chunk + 2 * two

        def o_fold(k):
            return remote(gbuf.at[span(odd(k), whole)], r.o0.at[span(k * whole, whole)], r.sem_o0, (k,), fold)

        def o_mirror(k):
            return remote(
                gbuf.at[span(odd(k) + (1 - m) * three, three)],
                r.o1.at[span(k * three, three)],
                r.sem_o1,
                (k,),
                mirror,
            )

        def o_half(k):
            return span(odd(k) + m * three, three)

        def o_rest(k):
            return span(odd(k) + (1 - m) * three, three)

        def o_side(k):
            return remote(
                gbuf.at[span(odd(k) + m * three + (1 - b) * six, six)],
                r.o2.at[span(k * six, six)],
                r.sem_o2,
                (k,),
                side,
            )

        def o_quarter(k):
            return span(odd(k) + m * three + b * six, six)

        def o_side_back(k):
            return remote(fbuf.at[o_quarter(k)], fbuf.at[o_quarter(k)], r.sem_o3, (k,), side)

        def o_mirror_back(k):
            return remote(fbuf.at[o_half(k)], fbuf.at[o_half(k)], r.sem_o4, (k,), mirror)

        def o_fold_back(k):
            return remote(fbuf.at[o_half(k)], fbuf.at[o_half(k)], r.sem_o5, (k,), fold)

        def o_fold_rest(k):
            return remote(fbuf.at[o_rest(k)], fbuf.at[o_rest(k)], r.sem_o6, (k,), fold)

        def e_step(e, k):
            if e == 0:
                e_side(k).wait_recv()
                add_into(gbuf, e_half(k), r.e0, span(k * two, two))

                @pl.when(end)
                def _():
                    e_fold(k).start()

            elif e == 1:

                @pl.when(middle)
                def _():
                    e_fold(k).wait_recv()
                    add_into(gbuf, e_half(k), r.e1, span(k * two, two))
                    e_mirror(k).start()

            elif e == 2:

                @pl.when(middle)
                def _():
                    e_mirror(k).wait_recv()
                    add_into(fbuf, e_quarter(k), r.e2, span(k * four, four))
                    e_mirror_back(k).start()

            elif e == 3:

                @pl.when(middle)
                def _():
                    e_mirror_back(k).wait_recv()
                    e_fold_back(k).start()
                    e_side_back(k).start()

            else:

                @pl.when(end)
                def _():
                    e_fold_back(k).wait_recv()
                    e_side_back(k).start()

        def o_step(e, k):
            @pl.when(middle)
            def _():
                if e == 0:
                    o_fold(k).wait_recv()
                    add_into(gbuf, span(odd(k), whole), r.o0, span(k * whole, whole))
                    o_mirror(k).start()
                elif e == 1:
                    o_mirror(k).wait_recv()
                    add_into(gbuf, o_half(k), r.o1, span(k * three, three))
                    o_side(k).start()
                elif e == 2:
                    o_side(k).wait_recv()
                    add_into(fbuf, o_quarter(k), r.o2, span(k * six, six))
                    o_side_back(k).start()
                elif e == 3:
                    o_side_back(k).wait_recv()
                    o_mirror_back(k).start()
                    o_fold_back(k).start()
                else:
                    o_mirror_back(k).wait_recv()
                    o_fold_rest(k).start()

        e_at = (0, 1, 2, 3, 5)
        o_at = (2, 3, 4, 5, 6)

        def o_first(k):
            @pl.when(end)
            def _():
                o_fold(k).start()

        def gradient_first(before, ready):
            for k in range(pairs):
                if before < (k + 1) * chunk <= ready:
                    e_side(k).start()

        def gradient_step(i):
            @pl.when(i < pairs)
            def _():
                o_first(i)

            for stage, places in ((o_step, o_at), (e_step, e_at)):
                for e, at in enumerate(places):

                    @pl.when((i >= at) & (i < at + pairs))
                    def _(stage=stage, e=e, at=at):
                        stage(e, i - at)

        def gradient_last(k):
            e_side_back(k).wait_recv()
            e_side(k).wait_send()
            e_side_back(k).wait_send()

            @pl.when(end)
            def _():
                o_fold_back(k).wait_recv()
                o_fold_rest(k).wait_recv()
                e_fold(k).wait_send()
                o_fold(k).wait_send()

            @pl.when(middle)
            def _():
                for make in (e_mirror, e_mirror_back, e_fold_back, o_mirror, o_side, o_side_back):
                    make(k).wait_send()
                for make in (o_mirror_back, o_fold_back, o_fold_rest):
                    make(k).wait_send()

        gradient_ticks = pairs + max(e_at[-1], o_at[-1])
        gradient_items = pairs
    else:
        def segment(k, t):
            start = k * chunk
            for u in range(t):
                start = start + dp_bit(u) * (chunk >> (u + 1))
            return start

        bases = [chunks * (chunk - (chunk >> t)) for t in range(bits)]

        def rs_at(k, t):
            size = chunk >> (t + 1)
            return span(bases[t] + k * size, size)

        def rs_send(k, t):
            size = chunk >> (t + 1)
            return remote(
                gbuf.at[span(segment(k, t) + (1 - dp_bit(t)) * size, size)],
                r.rbuf.at[rs_at(k, t)],
                r.sem_rs,
                (t, k),
                dp_peer(t),
            )

        def ag_send(k, t):
            at = span(segment(k, t + 1), chunk >> (t + 1))
            return remote(fbuf.at[at], fbuf.at[at], r.sem_ag, (t, k), dp_peer(t))

        def gradient_first(before, ready):
            for k in range(chunks):
                if before < (k + 1) * chunk <= ready:
                    rs_send(k, 0).start()

        def gradient_step(i):
            for e in reversed(range(2 * bits - 1)):
                k = i - e

                @pl.when((k >= 0) & (k < chunks))
                def _(e=e, k=k):
                    if e < bits:
                        rs_send(k, e).wait_recv()
                        at = span(segment(k, e + 1), chunk >> (e + 1))
                        add_into(gbuf if e + 1 < bits else fbuf, at, r.rbuf, rs_at(k, e))
                        if e + 1 < bits:
                            rs_send(k, e + 1).start()
                        else:
                            ag_send(k, e).start()
                    else:
                        t = 2 * bits - 1 - e
                        ag_send(k, t).wait_recv()
                        ag_send(k, t - 1).start()

        def gradient_last(k):
            ag_send(k, 0).wait_recv()
            for t in range(bits):
                rs_send(k, t).wait_send()
                ag_send(k, t).wait_send()

        gradient_ticks = chunks + 2 * bits - 2
        gradient_items = chunks

    t_half = tg.shape[0] // 2
    t_quarter = t_half // 2
    tc_keep = span(c * t_half, t_half)
    tc_give = span((1 - c) * t_half, t_half)
    tx_keep = span(x * t_quarter, t_quarter)
    tx_give = span((1 - x) * t_quarter, t_quarter)
    t_mine = span(c * t_half + x * t_quarter, t_quarter)
    tb, tcore, tcur, txr, tdp, trd, tall = r.tb, r.tcore, r.tcur, r.txr, r.tdp, r.trd, r.tall
    vcore, tfin = r.vcore, r.tfin
    t_core = remote(tb.at[tc_give], tcore, r.sem_t, (0,), core)
    t_across = remote(tcur.at[tx_give], txr, r.sem_t, (1,), across)
    t_back_x = remote(tall.at[t_mine], tall.at[t_mine], r.sem_t, (2,), across)
    t_back_c = remote(tall.at[tc_keep], tall.at[tc_keep], r.sem_t, (3,), core)
    v_core = remote(vg.at[pl.ds(0, 8)], vcore, r.sem_t, (4,), core)

    if folded:
        piece = tdp.shape[1] // n_dp
        steps_away = range(1, n_dp)

        def ahead(step):
            return (d + step) % n_dp

        def t_rs(step):
            return remote(
                tdp.at[0, span(ahead(step) * piece, piece)], trd.at[d], r.sem_tr, (step,), (ahead(step), s)
            )

        def t_ag(step):
            own_piece = span(d * piece, piece)
            return remote(tfin.at[own_piece], tfin.at[own_piece], r.sem_ta, (step,), (ahead(step), s))

        def t_spread():
            for step in steps_away:
                t_rs(step).start()

        def t_owned():
            for step in steps_away:
                t_rs(step).wait_recv()
            trd[d] = tdp[0, span(d * piece, piece)]
            total = trd[0].astype(F32)
            for at in range(1, n_dp):
                total = total + trd[at].astype(F32)
            tfin[span(d * piece, piece)] = total.astype(BF)
            for step in steps_away:
                t_ag(step).start()

        def t_whole():
            for step in steps_away:
                t_ag(step).wait_recv()

        t_exchange = [t_owned, t_whole]
        t_sends = [t_rs(step) for step in steps_away] + [t_ag(step) for step in steps_away]
        dp_peers = [(ahead(step), s) for step in steps_away]
    else:

        def t_dp(t):
            return remote(tdp.at[t], trd.at[t], r.sem_td, (t,), sum_peers[t])

        def t_spread():
            t_dp(0).start()

        def t_bit(t):
            t_dp(t).wait_recv()
            total = (tdp[t].astype(F32) + trd[t].astype(F32)).astype(BF)
            if t + 1 < bits:
                tdp[t + 1] = total
                t_dp(t + 1).start()
            else:
                tfin[...] = total

        t_exchange = [functools.partial(t_bit, t) for t in range(bits)]
        t_sends = [t_dp(t) for t in range(bits)]
        dp_peers = sum_peers

    barrier = pltpu.get_barrier_semaphore()
    peers = [core, across] + dp_peers
    for peer in peers:
        pl.semaphore_signal(barrier, inc=1, device_id=peer, device_id_type=MESH)

    small_names = names[3:13]
    smalls = [getattr(r, "in_" + n) for n in small_names]
    small_copies = [local(getattr(r, n), smalls[at], r.sem_small, at) for at, n in enumerate(small_names)]
    for copy in small_copies:
        copy.start()

    def start_local(j, carry):
        p_local(j).start()
        c_local(j).start()
        return carry

    lax.fori_loop(0, own, start_local, 0)
    for copy in weight_copies:
        copy.start()

    eye, wide = r.eye, r.wide
    eye[...] = jnp.where(diagonal(rows, count), 1.0, 0.0).astype(BF)
    wide[...] = jnp.where(diagonal(half, half), 1.0, 0.0).astype(BF)
    gci, gco, cib = r.gci, r.gco, r.cib
    gci[...] = jnp.zeros_like(gci)
    gco[...] = jnp.zeros_like(gco)
    cib[...] = jnp.zeros_like(cib)
    tg[...] = jnp.zeros_like(tg)
    vg[...] = jnp.zeros_like(vg)
    s2o[...] = jnp.zeros_like(s2o)
    s1o[...] = jnp.zeros_like(s1o)
    for copy in small_copies:
        copy.wait()
    vpad = r.vpad
    vpad[...] = jnp.zeros_like(vpad)
    for at in range(5):
        vpad[pl.ds(at, 1), pl.ds(0, width)] = smalls[at][...]
    vectors = vpad[...]
    r.vmine[...] = jnp.where(c == 0, vectors, pltpu.roll(vectors, width, 1))
    hidden_bias = r.hidden_row
    for at in range(hidden // LANE):
        hidden_bias[:, pl.ds(at * LANE, LANE)] = r.in_hidden_bias[pl.ds(at, 1), :]
    for at in range(toks // LANE):
        r.tok_row[:, pl.ds(at * LANE, LANE)] = r.in_tok_in_bias[pl.ds(at, 1), :]
    r.tib[...] = to_column(r.tok_row[...], toks)
    r.tob[...] = to_column(r.in_tok_out_bias[...], rows)
    tok_in_t, tok_in, tok_out, tok_out_t = r.tok_in_t, r.tok_in, r.tok_out, r.tok_out_t
    tok_in_t[...] = dot(eye[...], r.in_tok_in_raw[...]).astype(BF)
    tok_in[...] = dot_nt(wide[...], tok_in_t[...]).astype(BF)
    tok_out[...] = dot(eye[...], r.in_tok_out_raw[...]).astype(BF)
    tok_out_t[...] = dot_nt(wide[...], tok_out[...]).astype(BF)

    pl.semaphore_wait(barrier, len(peers))

    def start_images(j, carry):
        p_swap(j).start()
        c_swap(j).start()
        return carry

    v_swap.start()
    lax.fori_loop(0, own, start_images, 0)

    def turn_in(ref, j):
        return dot_nt(eye[...], ref[j])

    def turn_out(values):
        return dot_nt(wide[...], values)[:, :count].astype(BF)

    def merge_send(j):
        p_swap(j).wait_recv()
        p_local(j).wait()
        raw[j, :, near] = turn_in(pin, j).astype(BF)
        p_across(j).start()
        c_swap(j).wait_recv()
        c_local(j).wait()
        valid = jnp.where(c * own + j < r.counts[0], 1.0, 0.0)
        gb[j, first, near] = (turn_in(cin, j) * valid).astype(BF)
        c_across(j).start()

    merge_send(0)
    v_swap.wait_recv()
    vown[...] = r.vmine[...] + r.vpart[...]
    v_across.start()
    merge_send(1)
    merge_send(2)

    v_across.wait_recv()

    def vector(row):
        return jnp.concatenate([vown[pl.ds(row, 1), :], vother[pl.ds(row, 1), :]], axis=1)

    def normalise(values):
        centred = values - row_sum(values) * (1.0 / full)
        inverse = lax.rsqrt(row_sum(centred * centred) * (1.0 / full) + EPS)
        return centred * inverse, inverse

    def token_forward(j):
        values = raw[j].astype(F32)
        scaled, inverse = normalise(values)
        normed = (scaled * vector(0) + vector(1)).astype(BF)
        r.sc1[j] = scaled[:, :half].astype(BF)
        r.inv1[j] = inverse
        r.n1[j] = normed[:, :half]
        act, slope = gelu_parts(dot(tok_in[...], normed[:, :half]) + r.tib[...])
        r.tsl[j] = slope.astype(BF)
        act = act.astype(BF)
        r.ta[j] = act
        rest = gelu(dot(tok_in[...], normed[:, half:]) + r.tib[...]).astype(BF)
        mid = values + (dot(tok_out[...], jnp.concatenate([act, rest], axis=1)) + r.tob[...])
        r.mid[j] = mid[:, :half]
        scaled, inverse = normalise(mid)
        r.sc2[j] = scaled[:, :half].astype(BF)
        r.inv2[j] = inverse
        ntb[j, first] = (scaled * vector(2) + vector(3)).astype(BF)

    ghs, slopes = r.ghs, r.slopes
    step = 256

    def channel_front(j):
        nt = ntb[j]
        for at in range(hidden // step):
            cols = pl.ds(at * step, step)
            act, slope = gelu_parts(dot(nt, win[:, cols]) + hidden_bias[:, cols])
            outp[j, :, cols] = act.astype(BF)
            slopes[:, cols] = slope

    def channel_grads(j):
        g = gb[j]
        for at in range(hidden // step):
            cols = pl.ds(at * step, step)
            grad = (slopes[:, cols] * dot_nt(g, wout[cols, :])).astype(BF)
            ghs[:, cols] = grad
            cib[:, cols] += jnp.sum(grad.astype(F32), axis=0, keepdims=True)

    def channel_back(j):
        backp[j] = dot_nt(ghs[...], win[...]).astype(BF)
        back_pair(j).start()

    tiles = hidden // LANE

    def chan_out_grad(j, last):
        if last:
            for at in range(full // LANE):
                cols = pl.ds(at * LANE, LANE)
                total = gco[:, cols] + dot_tn(outp[j], gb[j, :, cols])
                gbuf[pl.ds(at * hidden, hidden)] = total.astype(BF)
        else:
            gco[...] += dot_tn(outp[j], gb[j])

    def chan_in_grad(j, last):
        if last:
            for at in range(tiles):
                cols = pl.ds(at * LANE, LANE)
                total = gci[:, cols] + dot_tn(ntb[j], ghs[:, cols])
                start = (full // LANE) * hidden + at * full
                gbuf[pl.ds(start, full)] = total.astype(BF)
        else:
            gci[...] += dot_tn(ntb[j], ghs[...])

    def pair_sums(j):
        back_pair(j).wait_recv()
        total = backp[j, first].astype(F32) + backr[j].astype(F32)
        s2o[j, pl.ds(0, 1)] = to_row(row_sum(total * vector(2)), rows)
        s2o[j, pl.ds(1, 1)] = to_row(row_sum(total * (ntb[j, first].astype(F32) - vector(3))), rows)
        backp[j, first] = total.astype(BF)
        s2_across(j).start()
        back_across(j).start()

    def gather_phase(j, carry):
        @pl.when(j + 3 < own)
        def _():
            merge_send(j + 3)

        p_across(j).wait_recv()
        token_forward(j)
        nt_share(j).start()

        @pl.when(j == 0)
        def _():
            for copy in weight_copies:
                copy.wait()

        @pl.when(j > 0)
        def _():
            g_share(j - 1).wait_recv()
            channel_grads(j - 1)
            channel_back(j - 1)
            chan_out_grad(j - 1, False)
            chan_in_grad(j - 1, False)

        c_across(j).wait_recv()
        g_share(j).start()
        nt_share(j).wait_recv()
        channel_front(j)

        @pl.when(j > 1)
        def _():
            pair_sums(j - 2)

        return carry

    lax.fori_loop(0, own, gather_phase, 0)

    g_share(own - 1).wait_recv()
    channel_grads(own - 1)
    chan_out_grad(own - 1, True)
    gradient_first(0, (full // LANE) * hidden)
    chan_in_grad(own - 1, True)
    gradient_first((full // LANE) * hidden, gbuf.shape[0])
    channel_back(own - 1)
    pair_sums(own - 2)
    pair_sums(own - 1)

    def partial_outs(j):
        outp[j] = dot(outp[j], wout[...]).astype(BF)
        out_pair(j).start()

    def pair_outs(j):
        out_pair(j).wait_recv()
        total = outp[j, first].astype(F32) + outr[j].astype(F32)
        outp[j, first] = total.astype(BF)
        out_across(j).start()

    def norm_back(weighted, scaled, inverse, sums):
        mean = to_column(sums[0:1] * (1.0 / full), rows)
        slant = to_column(sums[1:2] * (1.0 / full), rows)
        return inverse * (weighted - mean - scaled * slant)

    def token_backward(j):
        s2_across(j).wait_recv()
        back_across(j).wait_recv()
        grad_normed = backp[j, first, near].astype(F32) + backx[j].astype(F32)
        scaled = r.sc2[j].astype(F32)
        grad_out = gb[j, first, near].astype(F32)
        weighted = grad_normed * vown[pl.ds(2, 1), :]
        grad_mid = grad_out + norm_back(weighted, scaled, r.inv2[j], s2o[j] + s2x[j])
        r.gm[j] = grad_mid
        vg[pl.ds(2, 1), :] += jnp.sum(grad_normed * scaled, axis=0, keepdims=True)
        vg[pl.ds(3, 1), :] += jnp.sum(grad_normed, axis=0, keepdims=True)
        vg[pl.ds(4, 1), :] += jnp.sum(grad_out, axis=0, keepdims=True)
        low = grad_mid.astype(BF)
        ones = jnp.ones((8, half), BF)
        tg[pl.ds(rows, rows), :] += dot_nt(low, r.ta[j])
        tg[pl.ds(2 * rows + 8, 8), pl.ds(0, rows)] += dot_nt(ones, low)
        grad_pre = (r.tsl[j].astype(F32) * dot(tok_out_t[...], low)).astype(BF)
        tg[pl.ds(0, rows), :] += dot_nt(r.n1[j], grad_pre)
        tg[pl.ds(2 * rows, 8), :] += dot_nt(ones, grad_pre)
        grad_one = dot(tok_in_t[...], grad_pre)
        scaled = r.sc1[j].astype(F32)
        vg[pl.ds(0, 1), :] += jnp.sum(grad_one * scaled, axis=0, keepdims=True)
        vg[pl.ds(1, 1), :] += jnp.sum(grad_one, axis=0, keepdims=True)
        weighted = grad_one * vown[pl.ds(0, 1), :]
        r.w1[j] = weighted
        s1o[j, pl.ds(0, 1)] = to_row(row_sum(weighted), rows)
        s1o[j, pl.ds(1, 1)] = to_row(row_sum(weighted * scaled), rows)
        s1_across(j).start()

    def input_grad(j):
        s1_across(j).wait_recv()
        scaled = r.sc1[j].astype(F32)
        grad = r.gm[j] + norm_back(r.w1[j], scaled, r.inv1[j], s1o[j] + s1x[j])
        gis[j] = turn_out(grad.astype(BF))
        gin_give(j).start()
        gin_keep(j).start()

    def mixed_part(j):
        out_across(j).wait_recv()
        total = outp[j, first, near].astype(F32) + outx[j].astype(F32)
        valid = jnp.where(c * own + j < r.counts[0], 1.0, 0.0)
        mos[j] = turn_out((valid * (r.mid[j] + (total + vown[pl.ds(4, 1), :]))).astype(BF))
        mixed_give(j).start()
        mixed_keep(j).start()

    def token_start():
        tb[...] = tg[...].astype(BF)
        for at in range(hidden // half):
            vg[pl.ds(8 + at, 1), :] = cib[:, pl.ds(at * half, half)]
        t_core.start()
        v_core.start()

    def token_core():
        t_core.wait_recv()
        v_core.wait_recv()
        tcur[...] = (tb[tc_keep].astype(F32) + tcore[...].astype(F32)).astype(BF)
        t_across.start()
        vcore[...] = vg[pl.ds(0, 8)] + vcore[...]

    def token_across():
        t_across.wait_recv()
        tdp[0, pl.ds(0, t_quarter)] = (tcur[tx_keep].astype(F32) + txr[...].astype(F32)).astype(BF)
        tdp[0, pl.ds(t_quarter, 16)] = jnp.concatenate([vcore[...], vg[pl.ds(8, 8)]], axis=0).astype(BF)
        t_spread()

    def token_back():
        tall[t_mine] = tfin[pl.ds(0, t_quarter)]
        t_back_x.start()
        vec = tfin[pl.ds(t_quarter, 16)].astype(F32)
        vec_out[pl.ds(0, 8), :] = jnp.where(c == 0, vec, pltpu.roll(vec, width, 1))[:8]
        vec_out[pl.ds(8, 8), :] = vec[8:]

    def token_core_back():
        t_back_x.wait_recv()
        t_back_c.start()

    def token_end():
        t_back_c.wait_recv()
        vec_out[pl.ds(16, 16), :] = tall[pl.ds(2 * rows, 16)].astype(F32)

    token_steps = [token_start, token_core, None, token_across, None]
    for exchange in t_exchange[:-1]:
        token_steps += [exchange, None]

    def token_last():
        t_exchange[-1]()
        token_back()

    token_steps += [token_last, None, token_core_back, token_end]

    token_first = own - 1
    outs_first = 2
    mixed_first = own

    inputs_first = 4

    def scatter_phase(i, carry):
        gradient_step(i)

        def each(start, work):
            @pl.when((i >= start) & (i < start + own))
            def _():
                work(i - start)

        each(0, token_backward)
        for e, token_step in enumerate(token_steps):
            if token_step is not None:
                pl.when(i == token_first + e)(token_step)
        each(inputs_first, input_grad)
        each(outs_first, pair_outs)
        each(outs_first - 1, partial_outs)
        each(mixed_first, mixed_part)
        return carry

    lax.fori_loop(0, max(gradient_ticks, token_first + len(token_steps), mixed_first + own), scatter_phase, 0)

    def gradient_end(k, carry):
        gradient_last(k)
        return carry

    lax.fori_loop(0, gradient_items, gradient_end, 0)

    outs = []
    for at in range(full // LANE):
        to = mine if at < half // LANE else theirs
        lanes = pl.ds(pl.multiple_of(to + (at % (half // LANE)) * LANE, LANE), LANE)
        outs.append((fbuf.at[pl.ds(at * hidden, hidden)], r.g_chan_out.at[:, lanes]))
    for at in range(tiles):
        lanes = pl.ds(at * LANE, LANE)
        for part, to in enumerate((mine, theirs)):
            start = (full // LANE) * hidden + at * full + part * half
            outs.append((fbuf.at[pl.ds(start, half)], r.g_chan_in.at[pl.ds(to, half), lanes]))
    outs = [local(src, dst, r.sem_out, at) for at, (src, dst) in enumerate(outs)]
    for copy in outs:
        copy.start()

    def drain(j, carry):
        for make in (p_swap, c_swap, p_across, c_across, nt_share, g_share, out_pair, back_pair):
            make(j).wait_send()
        for make in (out_across, back_across, s2_across, s1_across):
            make(j).wait_send()
        for make in (mixed_give, gin_give, mixed_keep, gin_keep):
            make(j).wait()
        return carry

    lax.fori_loop(0, own, drain, 0)
    for copy in [v_swap, v_across, t_core, t_across, t_back_x, t_back_c, v_core] + t_sends:
        copy.wait_send()
    for copy in outs:
        copy.wait()


def run_layer(n_dp, **arrays):
    batch, width, count = arrays["patches"].shape
    own = batch // 2
    full, hidden = arrays["win_hbm"].shape
    half = full // 2
    toks = arrays["tok_in_raw"].shape[1]
    rows = -(-count // 16) * 16
    bits = n_dp.bit_length() - 1
    grad_rows = 2 * full * hidden // LANE
    folded = n_dp == 8
    choices = (8, 4, 2) if folded else (9, 3, 1)
    parts = 18 if folded else n_dp
    chunks = next(k for k in choices if grad_rows % (k * parts * (64 if folded else 16)) == 0)
    chunk = grad_rows // chunks
    cfg = (n_dp, own, count, rows, half, full, hidden, toks, chunks, chunk)
    vmem = pltpu.VMEM
    dma = pltpu.SemaphoreType.DMA
    two, whole = chunk * 13 // 36, chunk * 5 // 18
    t_rows = -(-(2 * rows + 16) // 64) * 64
    scratch = dict(
        win=vmem((full, hidden), BF),
        wout=vmem((hidden, full), BF),
        pin=vmem((own, half, count), BF),
        cin=vmem((own, half, count), BF),
        vpad=vmem((8, half), F32),
        hidden_row=vmem((1, hidden), F32),
        tok_row=vmem((1, toks), F32),
        vmine=vmem((8, half), F32),
        vpart=vmem((8, half), F32),
        vown=vmem((8, half), F32),
        vother=vmem((8, half), F32),
        eye=vmem((rows, count), BF),
        wide=vmem((half, half), BF),
        tok_in_t=vmem((rows, toks), BF),
        tok_in=vmem((toks, rows), BF),
        tok_out=vmem((rows, toks), BF),
        tok_out_t=vmem((toks, rows), BF),
        tib=vmem((toks, 1), F32),
        tob=vmem((rows, 1), F32),
        raw=vmem((own, rows, full), BF),
        ntb=vmem((own, 2 * rows, full), BF),
        gb=vmem((own, 2 * rows, full), BF),
        ghs=vmem((2 * rows, hidden), BF),
        slopes=vmem((2 * rows, hidden), F32),
        gci=vmem((full, hidden), F32),
        gco=vmem((hidden, full), F32),
        cib=vmem((1, hidden), F32),
        outp=vmem((own, 2 * rows, full), BF),
        outr=vmem((own, rows, full), BF),
        backp=vmem((own, 2 * rows, full), BF),
        backr=vmem((own, rows, full), BF),
        outx=vmem((own, rows, half), BF),
        backx=vmem((own, rows, half), BF),
        s2o=vmem((own, 8, rows), F32),
        s2x=vmem((own, 8, rows), F32),
        s1o=vmem((own, 8, rows), F32),
        s1x=vmem((own, 8, rows), F32),
        n1=vmem((own, rows, half), BF),
        ta=vmem((own, toks, half), BF),
        tsl=vmem((own, toks, half), BF),
        mid=vmem((own, rows, half), F32),
        sc1=vmem((own, rows, half), BF),
        sc2=vmem((own, rows, half), BF),
        inv1=vmem((own, rows, 1), F32),
        inv2=vmem((own, rows, 1), F32),
        gm=vmem((own, rows, half), F32),
        w1=vmem((own, rows, half), F32),
        gbuf=vmem((grad_rows, LANE), BF),
        fbuf=vmem((grad_rows, LANE), BF),
        tg=vmem((t_rows, toks), F32),
        tb=vmem((t_rows, toks), BF),
        tcore=vmem((t_rows // 2, toks), BF),
        tcur=vmem((t_rows // 2, toks), BF),
        txr=vmem((t_rows // 4, toks), BF),
        tdp=vmem((1 if folded else bits, t_rows // 4 + 16, toks), BF),
        trd=vmem((n_dp, (t_rows // 4 + 16) // n_dp, toks) if folded else (bits, t_rows // 4 + 16, toks), BF),
        tfin=vmem((t_rows // 4 + 16, toks), BF),
        vg=vmem((16, half), F32),
        vcore=vmem((8, half), F32),
        sem_w=dma((4,)),
        sem_small=dma((10,)),
        sem_v=dma((2, 2)),
        sem_out=dma((2 * (hidden // LANE) + full // LANE,)),
        sem_t=dma((2, 5)),
        sem_td=dma((2, bits)),
        sem_tr=dma((2, n_dp)),
        sem_ta=dma((2, n_dp)),
    )
    for name in list(arrays)[3:13]:
        scratch["in_" + name] = vmem(arrays[name].shape, arrays[name].dtype)
    for name in ("pl", "cl", "mk", "gk"):
        scratch["sem_" + name] = dma((own,))
    for name in ("ps", "cs", "px", "cx", "nt", "g", "op", "bp", "ox", "bx", "s2", "s1", "mg", "gg"):
        scratch["sem_" + name] = dma((2, own))
    if folded:
        scratch["e0"] = vmem((chunks * two, LANE), BF)
        scratch["e1"] = vmem((chunks * two, LANE), BF)
        scratch["e2"] = vmem((chunks * two // 2, LANE), BF)
        scratch["o0"] = vmem((chunks * whole, LANE), BF)
        scratch["o1"] = vmem((chunks * whole // 2, LANE), BF)
        scratch["o2"] = vmem((chunks * whole // 4, LANE), BF)
        for name in [e + str(k) for e in "eo" for k in range(7)]:
            scratch["sem_" + name] = dma((2, chunks))
    else:
        scratch["rbuf"] = vmem((chunks * (chunk - (chunk >> bits)), LANE), BF)
        scratch["sem_rs"] = dma((2, bits, chunks))
        scratch["sem_ag"] = dma((2, bits, chunks))
    hbm = pl.BlockSpec(memory_space=pl.ANY)
    inside = pl.BlockSpec(memory_space=pltpu.VMEM)
    places = dict(counts=pl.BlockSpec(memory_space=pltpu.SMEM), tall=inside, vec_out=inside)
    outs = dict(
        mixed=((batch, width, count), BF),
        gin=((batch, width, count), BF),
        tall=((t_rows, toks), BF),
        vec_out=((32, half), F32),
        g_chan_in=((full, hidden), BF),
        g_chan_out=((hidden, full), BF),
    )
    names = list(arrays) + list(outs) + list(scratch)
    results = pl.pallas_call(
        functools.partial(layer_kernel, cfg, names),
        out_shape=tuple(jax.ShapeDtypeStruct(*outs[name]) for name in outs),
        in_specs=[places.get(name, hbm) for name in arrays],
        out_specs=tuple(places.get(name, hbm) for name in outs),
        scratch_shapes=list(scratch.values()),
        compiler_params=pltpu.CompilerParams(
            collective_id=0, has_side_effects=True, vmem_limit_bytes=63 * 2**20
        ),
        name="mixer_layer",
    )(*arrays.values())
    return SimpleNamespace(**dict(zip(outs, results)))


def finish_kernel(names, *refs):
    r = SimpleNamespace(**dict(zip(names, refs)))
    sems = r.sems
    count, toks = r.tok_in.shape
    rows = -(-count // 16) * 16
    parts = r.pieces.shape[1]
    step = r.pieces.shape[2]
    loads, stores = [], []
    whole_in, whole_out = [], []
    for at, (raw, done) in enumerate(((r.mixed_raw, r.mixed), (r.gin_raw, r.gin))):
        for part in range(2):
            here = pl.ds(part * (r.images.shape[1] // 2), r.images.shape[1] // 2)
            sem = 2 + 4 * parts + 4 * at + 2 * part
            whole_in.append(pltpu.make_async_copy(raw.at[here], r.images.at[at, here], sems.at[sem]))
            whole_out.append(pltpu.make_async_copy(r.images.at[at, here], done.at[here], sems.at[sem + 1]))
    for at, (raw, done) in enumerate(((r.chan_in_raw, r.chan_in), (r.chan_out_raw, r.chan_out))):
        for part in range(parts):
            here = pl.ds(part * step, step)
            sem = 2 + at * parts + part
            loads.append(pltpu.make_async_copy(raw.at[here], r.pieces.at[at, part], sems.at[sem]))
            stores.append(
                pltpu.make_async_copy(r.wide.at[at, part], done.at[here], sems.at[sem + 2 * parts])
            )
    for copy in loads + whole_in:
        copy.start()
    for at in range(len(loads)):
        loads[at].wait()
        r.wide[at // parts, at % parts] = r.pieces[at // parts, at % parts].astype(F32)
        stores[at].start()
    for at in range(len(whole_in)):
        whole_in[at].wait()
        whole_out[at].start()
    vec, tall = r.vec_raw, r.tok_raw
    width = r.ln1_gain.shape[1]
    for at, done in enumerate((r.ln1_gain, r.ln1_bias, r.ln2_gain, r.ln2_bias, r.chan_out_bias)):
        done[...] = vec[pl.ds(at, 1), :][:, :width]
    half = vec.shape[1]
    for at in range(r.chan_in_bias.shape[0]):
        row, lane = divmod(at * LANE, half)
        r.chan_in_bias[pl.ds(at, 1), :] = vec[pl.ds(8 + row, 1), pl.ds(lane, LANE)]
    for at in range(toks // LANE):
        r.tok_in_bias[pl.ds(at, 1), :] = vec[pl.ds(16, 1), pl.ds(at * LANE, LANE)]
    r.tok_out_bias[...] = vec[pl.ds(24, 1), :][:, :count]
    r.tok_in[...] = tall[pl.ds(0, rows)][:count].astype(F32)
    r.tok_out[...] = tall[pl.ds(rows, rows)][:count].astype(F32)
    for copy in stores + whole_out:
        copy.wait()


def finish(out, count, width):
    full, hidden = out.g_chan_in.shape
    toks = out.tall.shape[1]
    hbm = pl.BlockSpec(memory_space=pl.ANY)
    inside = pl.BlockSpec(memory_space=pltpu.VMEM)
    arrays = dict(
        mixed_raw=out.mixed,
        gin_raw=out.gin,
        chan_in_raw=out.g_chan_in,
        chan_out_raw=out.g_chan_out,
        tok_raw=out.tall,
        vec_raw=out.vec_out,
    )
    outs = dict(
        mixed=(out.mixed.shape, BF),
        gin=(out.gin.shape, BF),
        chan_in=((full, hidden), F32),
        chan_out=((hidden, full), F32),
        ln1_gain=((1, width), F32),
        ln1_bias=((1, width), F32),
        ln2_gain=((1, width), F32),
        ln2_bias=((1, width), F32),
        chan_out_bias=((1, width), F32),
        chan_in_bias=((hidden // LANE, LANE), F32),
        tok_in_bias=((toks // LANE, LANE), F32),
        tok_out_bias=((1, count), F32),
        tok_in=((count, toks), F32),
        tok_out=((count, toks), F32),
    )
    parts = 4
    scratch = dict(
        pieces=pltpu.VMEM((2, parts, full // parts, hidden), BF),
        wide=pltpu.VMEM((2, parts, full // parts, hidden), F32),
        images=pltpu.VMEM((2,) + out.mixed.shape, BF),
        sems=pltpu.SemaphoreType.DMA((10 + 4 * parts,)),
    )
    names = list(arrays) + list(outs) + list(scratch)
    results = pl.pallas_call(
        functools.partial(finish_kernel, names),
        out_shape=tuple(jax.ShapeDtypeStruct(*outs[name]) for name in outs),
        in_specs=[hbm] * 4 + [inside] * 2,
        out_specs=(hbm,) * 4 + (inside,) * 10,
        scratch_shapes=list(scratch.values()),
        compiler_params=pltpu.CompilerParams(vmem_limit_bytes=63 * 2**20),
        name="finish",
    )(*arrays.values())
    return SimpleNamespace(**dict(zip(outs, results)))


def per_device(
    n_dp,
    image_counts,
    patches,
    ln1_gain,
    ln1_bias,
    tok_in_weight,
    tok_in_bias,
    tok_out_weight,
    tok_out_bias,
    ln2_gain,
    ln2_bias,
    chan_in_weight,
    chan_in_bias,
    chan_out_weight,
    chan_out_bias,
    cotangent,
):
    out = run_layer(
        n_dp,
        counts=image_counts,
        patches=jnp.transpose(patches, (1, 2, 0)),
        cot=jnp.transpose(cotangent, (1, 2, 0)),
        ln1_gain=ln1_gain[None, :],
        ln1_bias=ln1_bias[None, :],
        ln2_gain=ln2_gain[None, :],
        ln2_bias=ln2_bias[None, :],
        chan_out_bias=chan_out_bias[None, :],
        hidden_bias=chan_in_bias.reshape(-1, LANE),
        tok_in_bias=tok_in_bias.reshape(-1, LANE),
        tok_out_bias=tok_out_bias[None, :],
        tok_in_raw=tok_in_weight.T,
        tok_out_raw=tok_out_weight,
        win_hbm=chan_in_weight,
        wout_hbm=chan_out_weight,
    )
    out = finish(out, patches.shape[0], patches.shape[2])
    return (
        jnp.transpose(out.mixed, (2, 0, 1)),
        jnp.transpose(out.gin, (2, 0, 1)),
        out.ln1_gain[0],
        out.ln1_bias[0],
        out.tok_in.T,
        out.tok_in_bias.reshape(-1),
        out.tok_out,
        out.tok_out_bias[0],
        out.ln2_gain[0],
        out.ln2_bias[0],
        out.chan_in,
        out.chan_in_bias.reshape(-1),
        out.chan_out,
        out.chan_out_bias[0],
    )


def solution(mesh):
    in_specs = (
        P("dp"),
        P(None, "dp", "seq"),
        P("seq"),
        P("seq"),
        P(),
        P(),
        P(),
        P(),
        P("seq"),
        P("seq"),
        P(None, "seq"),
        P("seq"),
        P("seq", None),
        P("seq"),
        P(None, "dp", "seq"),
    )
    out_specs = (
        P(None, "dp", "seq"),
        P(None, "dp", "seq"),
        P("seq"),
        P("seq"),
        P(),
        P(),
        P(),
        P(),
        P("seq"),
        P("seq"),
        P(None, "seq"),
        P("seq"),
        P("seq", None),
        P("seq"),
    )
    return jax.shard_map(
        functools.partial(per_device, mesh.shape["dp"]),
        mesh=mesh,
        in_specs=in_specs,
        out_specs=out_specs,
        check_vma=False,
    )
```

time: 144 us -> 130 us (0.903)
  Pallas kernels: 142 us -> 128 us
    pallas_call x1, Pallas kernels: 136 us -> 122 us  [run_layer(): pl.pallas_call(functools.partial(layer_kernel, cfg, names), out_shape=tup...]
where the time goes in v3:
time: 130 us
  Pallas kernels  128 us (98%)
  between operations  1.46 us (1%)
    pallas_call x1, Pallas kernels, run_layer(): pl.pallas_call(functools.partial(layer_kernel, cfg, names), out_shape=tup...  122 us
    pallas_call x1, Pallas kernels, finish(): pl.pallas_call(functools.partial(finish_kernel, names), out_shape=tuple((...  6.19 us

profile of v3, /device:TPU:0, one launch (start us, length us, event | category | flops | bytes accessed | tf_op | source)
XLA Modules:
  0.0 129.7 jit_solution(18354086239083014278)
XLA Ops:
  1.3 122.1 %mixer_layer.1 = (bf16[12,192,196]{2,1,0:T(8,128)(2,1)}, bf16[12,192,196]{2,1,0:T(8,128)(2,1)}, bf16[448,384]{1,0:T(8,128)(2,1)}, f32[32,384]{1,0:T(8,128)}, bf1...) custom-call(s32[1]{0:T(128)S(6)} %copy.29.refs_0_, bf16[12,192,196]{2,1,0:T(8,128)(2,1)} %bitcast.22, ...), custom_call_target="tpu_custom_call" | custom-call | tf_op jit(solution)/shard_map/mixer_layer/pallas_call | solution.py:1022
  123.4 6.2 %finish.1 = (bf16[12,192,196]{2,1,0:T(8,128)(2,1)}, bf16[12,192,196]{2,1,0:T(8,128)(2,1)}, f32[768,768]{1,0:T(8,128)}, f32[768,768]{1,0:T(8,128)}, f32[1,192]{1,...) custom-call(bf16[12,192,196]{2,1,0:T(8,128)(2,1)} %get-tuple-element, ...), custom_call_target="tpu_custom_call" | custom-call | tf_op jit(solution)/shard_map/finish/pallas_call | solution.py:1122

commit v4 on v3

--- a/solution.py
+++ b/solution.py
@@ -193,7 +193,7 @@
 
     if folded:
         pairs = chunks
-        two, four = chunk * 13 // 36, chunk * 13 // 72
+        two, four = chunk * 14 // 36, chunk * 14 // 72
 
         def even(k):
             return k * chunk
@@ -230,7 +230,7 @@
         def e_side_back(k):
             return remote(fbuf.at[e_half(k)], fbuf.at[e_half(k)], r.sem_e5, (k,), side)
 
-        whole, three, six = chunk * 5 // 18, chunk * 5 // 36, chunk * 5 // 72
+        whole, three, six = chunk * 4 // 18, chunk * 4 // 36, chunk * 4 // 72
 
         def odd(k):
             return k * chunk + 2 * two
@@ -340,8 +340,8 @@
                     o_mirror_back(k).wait_recv()
                     o_fold_rest(k).start()
 
-        e_at = (0, 1, 2, 3, 5)
-        o_at = (2, 3, 4, 5, 6)
+        e_at = (1, 2, 3, 4, 6)
+        o_at = (1, 3, 5, 6, 7)
 
         def o_first(k):
             @pl.when(end)
@@ -367,13 +367,18 @@
 
         def gradient_last(k):
             e_side_back(k).wait_recv()
-            e_side(k).wait_send()
-            e_side_back(k).wait_send()
 
             @pl.when(end)
             def _():
                 o_fold_back(k).wait_recv()
                 o_fold_rest(k).wait_recv()
+
+        def gradient_sent(k):
+            e_side(k).wait_send()
+            e_side_back(k).wait_send()
+
+            @pl.when(end)
+            def _():
                 e_fold(k).wait_send()
                 o_fold(k).wait_send()
 
@@ -439,6 +444,8 @@
 
         def gradient_last(k):
             ag_send(k, 0).wait_recv()
+
+        def gradient_sent(k):
             for t in range(bits):
                 rs_send(k, t).wait_send()
                 ag_send(k, t).wait_send()
@@ -540,25 +547,49 @@
     for copy in weight_copies:
         copy.start()
 
-    eye, wide = r.eye, r.wide
+    eye, wide, vpad = r.eye, r.wide, r.vpad
     eye[...] = jnp.where(diagonal(rows, count), 1.0, 0.0).astype(BF)
-    wide[...] = jnp.where(diagonal(half, half), 1.0, 0.0).astype(BF)
-    gci, gco, cib = r.gci, r.gco, r.cib
-    gci[...] = jnp.zeros_like(gci)
-    gco[...] = jnp.zeros_like(gco)
-    cib[...] = jnp.zeros_like(cib)
-    tg[...] = jnp.zeros_like(tg)
-    vg[...] = jnp.zeros_like(vg)
-    s2o[...] = jnp.zeros_like(s2o)
-    s1o[...] = jnp.zeros_like(s1o)
+    vpad[...] = jnp.zeros_like(vpad)
     for copy in small_copies:
         copy.wait()
-    vpad = r.vpad
-    vpad[...] = jnp.zeros_like(vpad)
     for at in range(5):
         vpad[pl.ds(at, 1), pl.ds(0, width)] = smalls[at][...]
     vectors = vpad[...]
     r.vmine[...] = jnp.where(c == 0, vectors, pltpu.roll(vectors, width, 1))
+
+    pl.semaphore_wait(barrier, len(peers))
+
+    def start_images(j, carry):
+        p_swap(j).start()
+        c_swap(j).start()
+        return carry
+
+    v_swap.start()
+    lax.fori_loop(0, own, start_images, 0)
+
+    def turn_in(ref, j):
+        return dot_nt(eye[...], ref[j])
+
+    def turn_out(values):
+        return dot_nt(wide[...], values)[:, :count].astype(BF)
+
+    def merge_send(j):
+        p_swap(j).wait_recv()
+        p_local(j).wait()
+        raw[j, :, near] = turn_in(pin, j).astype(BF)
+        p_across(j).start()
+        c_swap(j).wait_recv()
+        c_local(j).wait()
+        valid = jnp.where(c * own + j < r.counts[0], 1.0, 0.0)
+        gb[j, first, near] = (turn_in(cin, j) * valid).astype(BF)
+        c_across(j).start()
+
+    v_swap.wait_recv()
+    vown[...] = r.vmine[...] + r.vpart[...]
+    v_across.start()
+    merge_send(0)
+
+    wide[...] = jnp.where(diagonal(half, half), 1.0, 0.0).astype(BF)
     hidden_bias = r.hidden_row
     for at in range(hidden // LANE):
         hidden_bias[:, pl.ds(at * LANE, LANE)] = r.in_hidden_bias[pl.ds(at, 1), :]
@@ -571,41 +602,16 @@
     tok_in[...] = dot_nt(wide[...], tok_in_t[...]).astype(BF)
     tok_out[...] = dot(eye[...], r.in_tok_out_raw[...]).astype(BF)
     tok_out_t[...] = dot_nt(wide[...], tok_out[...]).astype(BF)
-
-    pl.semaphore_wait(barrier, len(peers))
-
-    def start_images(j, carry):
-        p_swap(j).start()
-        c_swap(j).start()
-        return carry
-
-    v_swap.start()
-    lax.fori_loop(0, own, start_images, 0)
-
-    def turn_in(ref, j):
-        return dot_nt(eye[...], ref[j])
-
-    def turn_out(values):
-        return dot_nt(wide[...], values)[:, :count].astype(BF)
-
-    def merge_send(j):
-        p_swap(j).wait_recv()
-        p_local(j).wait()
-        raw[j, :, near] = turn_in(pin, j).astype(BF)
-        p_across(j).start()
-        c_swap(j).wait_recv()
-        c_local(j).wait()
-        valid = jnp.where(c * own + j < r.counts[0], 1.0, 0.0)
-        gb[j, first, near] = (turn_in(cin, j) * valid).astype(BF)
-        c_across(j).start()
-
-    merge_send(0)
-    v_swap.wait_recv()
-    vown[...] = r.vmine[...] + r.vpart[...]
-    v_across.start()
     merge_send(1)
+    gci, gco, cib = r.gci, r.gco, r.cib
+    gci[...] = jnp.zeros_like(gci)
+    gco[...] = jnp.zeros_like(gco)
+    cib[...] = jnp.zeros_like(cib)
+    tg[...] = jnp.zeros_like(tg)
+    vg[...] = jnp.zeros_like(vg)
+    s2o[...] = jnp.zeros_like(s2o)
+    s1o[...] = jnp.zeros_like(s1o)
     merge_send(2)
-
     v_across.wait_recv()
 
     def vector(row):
@@ -646,16 +652,16 @@
             outp[j, :, cols] = act.astype(BF)
             slopes[:, cols] = slope
 
-    def channel_grads(j):
-        g = gb[j]
+    def channel_grads(j, part):
+        g = gb[j, part]
         for at in range(hidden // step):
             cols = pl.ds(at * step, step)
-            grad = (slopes[:, cols] * dot_nt(g, wout[cols, :])).astype(BF)
-            ghs[:, cols] = grad
+            grad = (slopes[part, cols] * dot_nt(g, wout[cols, :])).astype(BF)
+            ghs[j % 2, part, cols] = grad
             cib[:, cols] += jnp.sum(grad.astype(F32), axis=0, keepdims=True)
 
     def channel_back(j):
-        backp[j] = dot_nt(ghs[...], win[...]).astype(BF)
+        backp[j] = dot_nt(ghs[j % 2], win[...]).astype(BF)
         back_pair(j).start()
 
     tiles = hidden // LANE
@@ -673,11 +679,11 @@
         if last:
             for at in range(tiles):
                 cols = pl.ds(at * LANE, LANE)
-                total = gci[:, cols] + dot_tn(ntb[j], ghs[:, cols])
+                total = gci[:, cols] + dot_tn(ntb[j], ghs[j % 2, :, cols])
                 start = (full // LANE) * hidden + at * full
                 gbuf[pl.ds(start, full)] = total.astype(BF)
         else:
-            gci[...] += dot_tn(ntb[j], ghs[...])
+            gci[...] += dot_tn(ntb[j], ghs[j % 2])
 
     def pair_sums(j):
         back_pair(j).wait_recv()
@@ -705,9 +711,15 @@
         @pl.when(j > 0)
         def _():
             g_share(j - 1).wait_recv()
-            channel_grads(j - 1)
+            channel_grads(j - 1, pl.ds(0, 2 * rows))
+            chan_out_grad(j - 1, False)
+
+        @pl.when(j > 0)
+        def _():
             channel_back(j - 1)
-            chan_out_grad(j - 1, False)
+
+        @pl.when((j > 0) & (j < own - 1))
+        def _():
             chan_in_grad(j - 1, False)
 
         c_across(j).wait_recv()
@@ -715,7 +727,7 @@
         nt_share(j).wait_recv()
         channel_front(j)
 
-        @pl.when(j > 1)
+        @pl.when((j > 1) & (j < own - 1))
         def _():
             pair_sums(j - 2)
 
@@ -723,16 +735,14 @@
 
     lax.fori_loop(0, own, gather_phase, 0)
 
+    channel_grads(own - 1, first)
     g_share(own - 1).wait_recv()
-    channel_grads(own - 1)
+    channel_grads(own - 1, second)
     chan_out_grad(own - 1, True)
     gradient_first(0, (full // LANE) * hidden)
+    chan_in_grad(own - 2, False)
     chan_in_grad(own - 1, True)
     gradient_first((full // LANE) * hidden, gbuf.shape[0])
-    channel_back(own - 1)
-    pair_sums(own - 2)
-    pair_sums(own - 1)
-
     def partial_outs(j):
         outp[j] = dot(outp[j], wout[...]).astype(BF)
         out_pair(j).start()
@@ -824,9 +834,13 @@
         t_back_x.wait_recv()
         t_back_c.start()
 
+    token_outs = [local(tall, r.tok_grads, r.sem_tok, 0), local(vec_out, r.vec_grads, r.sem_tok, 1)]
+
     def token_end():
         t_back_c.wait_recv()
         vec_out[pl.ds(16, 16), :] = tall[pl.ds(2 * rows, 16)].astype(F32)
+        for copy in token_outs:
+            copy.start()
 
     token_steps = [token_start, token_core, None, token_across, None]
     for exchange in t_exchange[:-1]:
@@ -842,7 +856,7 @@
     outs_first = 2
     mixed_first = own
 
-    inputs_first = 4
+    inputs_first = 5
 
     def scatter_phase(i, carry):
         gradient_step(i)
@@ -851,6 +865,15 @@
             @pl.when((i >= start) & (i < start + own))
             def _():
                 work(i - start)
+
+        @pl.when(i == 0)
+        def _():
+            channel_back(own - 1)
+
+        @pl.when(i == 1)
+        def _():
+            for j in range(own - 3, own):
+                pair_sums(j)
 
         each(0, token_backward)
         for e, token_step in enumerate(token_steps):
@@ -864,25 +887,28 @@
 
     lax.fori_loop(0, max(gradient_ticks, token_first + len(token_steps), mixed_first + own), scatter_phase, 0)
 
-    def gradient_end(k, carry):
-        gradient_last(k)
-        return carry
-
-    lax.fori_loop(0, gradient_items, gradient_end, 0)
-
     outs = []
     for at in range(full // LANE):
         to = mine if at < half // LANE else theirs
         lanes = pl.ds(pl.multiple_of(to + (at % (half // LANE)) * LANE, LANE), LANE)
-        outs.append((fbuf.at[pl.ds(at * hidden, hidden)], r.g_chan_out.at[:, lanes]))
+        here = pl.ds(at * hidden, hidden)
+        outs.append((here, local(fbuf.at[here], r.g_chan_out.at[:, lanes], r.sem_out, len(outs))))
     for at in range(tiles):
         lanes = pl.ds(at * LANE, LANE)
         for part, to in enumerate((mine, theirs)):
-            start = (full // LANE) * hidden + at * full + part * half
-            outs.append((fbuf.at[pl.ds(start, half)], r.g_chan_in.at[pl.ds(to, half), lanes]))
-    outs = [local(src, dst, r.sem_out, at) for at, (src, dst) in enumerate(outs)]
-    for copy in outs:
-        copy.start()
+            here = pl.ds((full // LANE) * hidden + at * full + part * half, half)
+            outs.append((here, local(fbuf.at[here], r.g_chan_in.at[pl.ds(to, half), lanes], r.sem_out, len(outs))))
+    for k in range(gradient_items):
+        gradient_last(k)
+        for here, copy in outs:
+            if k * chunk < here.start + here.size <= (k + 1) * chunk:
+                copy.start()
+
+    def gradient_drain(k, carry):
+        gradient_sent(k)
+        return carry
+
+    lax.fori_loop(0, gradient_items, gradient_drain, 0)
 
     def drain(j, carry):
         for make in (p_swap, c_swap, p_across, c_across, nt_share, g_share, out_pair, back_pair):
@@ -896,7 +922,9 @@
     lax.fori_loop(0, own, drain, 0)
     for copy in [v_swap, v_across, t_core, t_across, t_back_x, t_back_c, v_core] + t_sends:
         copy.wait_send()
-    for copy in outs:
+    for _, copy in outs:
+        copy.wait()
+    for copy in token_outs:
         copy.wait()
 
 
@@ -917,7 +945,7 @@
     cfg = (n_dp, own, count, rows, half, full, hidden, toks, chunks, chunk)
     vmem = pltpu.VMEM
     dma = pltpu.SemaphoreType.DMA
-    two, whole = chunk * 13 // 36, chunk * 5 // 18
+    two, whole = chunk * 14 // 36, chunk * 4 // 18
     t_rows = -(-(2 * rows + 16) // 64) * 64
     scratch = dict(
         win=vmem((full, hidden), BF),
@@ -942,7 +970,7 @@
         raw=vmem((own, rows, full), BF),
         ntb=vmem((own, 2 * rows, full), BF),
         gb=vmem((own, 2 * rows, full), BF),
-        ghs=vmem((2 * rows, hidden), BF),
+        ghs=vmem((2, 2 * rows, hidden), BF),
         slopes=vmem((2 * rows, hidden), F32),
         gci=vmem((full, hidden), F32),
         gco=vmem((hidden, full), F32),
@@ -976,6 +1004,9 @@
         txr=vmem((t_rows // 4, toks), BF),
         tdp=vmem((1 if folded else bits, t_rows // 4 + 16, toks), BF),
         trd=vmem((n_dp, (t_rows // 4 + 16) // n_dp, toks) if folded else (bits, t_rows // 4 + 16, toks), BF),
+        tall=vmem((t_rows, toks), BF),
+        vec_out=vmem((32, half), F32),
+        sem_tok=dma((2,)),
         tfin=vmem((t_rows // 4 + 16, toks), BF),
         vg=vmem((16, half), F32),
         vcore=vmem((8, half), F32),
@@ -1008,13 +1039,12 @@
         scratch["sem_rs"] = dma((2, bits, chunks))
         scratch["sem_ag"] = dma((2, bits, chunks))
     hbm = pl.BlockSpec(memory_space=pl.ANY)
-    inside = pl.BlockSpec(memory_space=pltpu.VMEM)
-    places = dict(counts=pl.BlockSpec(memory_space=pltpu.SMEM), tall=inside, vec_out=inside)
+    places = dict(counts=pl.BlockSpec(memory_space=pltpu.SMEM))
     outs = dict(
         mixed=((batch, width, count), BF),
         gin=((batch, width, count), BF),
-        tall=((t_rows, toks), BF),
-        vec_out=((32, half), F32),
+        tok_grads=((t_rows, toks), BF),
+        vec_grads=((32, half), F32),
         g_chan_in=((full, hidden), BF),
         g_chan_out=((hidden, full), BF),
     )
@@ -1033,73 +1063,91 @@
     return SimpleNamespace(**dict(zip(outs, results)))
 
 
-def finish_kernel(names, *refs):
+def finish_kernel(names, smalls, *refs):
     r = SimpleNamespace(**dict(zip(names, refs)))
-    sems = r.sems
     count, toks = r.tok_in.shape
     rows = -(-count // 16) * 16
-    parts = r.pieces.shape[1]
-    step = r.pieces.shape[2]
+    parts, step = r.pieces.shape[1:3]
+    images = r.images.shape[1] // 2
+
+    def copy(src, dst, at):
+        return pltpu.make_async_copy(src, dst, r.sems.at[at])
+
     loads, stores = [], []
-    whole_in, whole_out = [], []
+    for at, (raw, done) in enumerate(((r.chan_out_raw, r.chan_out), (r.chan_in_raw, r.chan_in))):
+        for part in range(parts):
+            here = pl.ds(part * step, step)
+            loads.append(copy(raw.at[here], r.pieces.at[at, part], len(loads)))
+            stores.append(copy(r.wide.at[at, part], done.at[here], 2 * parts + len(stores)))
+    first = 4 * parts
+    images_in, images_out = [], []
     for at, (raw, done) in enumerate(((r.mixed_raw, r.mixed), (r.gin_raw, r.gin))):
         for part in range(2):
-            here = pl.ds(part * (r.images.shape[1] // 2), r.images.shape[1] // 2)
-            sem = 2 + 4 * parts + 4 * at + 2 * part
-            whole_in.append(pltpu.make_async_copy(raw.at[here], r.images.at[at, here], sems.at[sem]))
-            whole_out.append(pltpu.make_async_copy(r.images.at[at, here], done.at[here], sems.at[sem + 1]))
-    for at, (raw, done) in enumerate(((r.chan_in_raw, r.chan_in), (r.chan_out_raw, r.chan_out))):
-        for part in range(parts):
-            here = pl.ds(part * step, step)
-            sem = 2 + at * parts + part
-            loads.append(pltpu.make_async_copy(raw.at[here], r.pieces.at[at, part], sems.at[sem]))
-            stores.append(
-                pltpu.make_async_copy(r.wide.at[at, part], done.at[here], sems.at[sem + 2 * parts])
-            )
-    for copy in loads + whole_in:
-        copy.start()
-    for at in range(len(loads)):
+            here = pl.ds(part * images, images)
+            images_in.append(copy(raw.at[here], r.images.at[at, here], first + len(images_in)))
+            images_out.append(copy(r.images.at[at, here], done.at[here], first + 4 + len(images_out)))
+    first += 8
+    tok_load = copy(r.tok_raw, r.tall, first)
+    vec_load = copy(r.vec_raw, r.vec, first + 1)
+    small_stores = [
+        copy(getattr(r, "out_" + name), getattr(r, name), first + 2 + at) for at, name in enumerate(smalls)
+    ]
+    for load in loads[:2] + [tok_load, vec_load] + loads[2:] + images_in:
+        load.start()
+
+    def widen(at):
         loads[at].wait()
         r.wide[at // parts, at % parts] = r.pieces[at // parts, at % parts].astype(F32)
         stores[at].start()
-    for at in range(len(whole_in)):
-        whole_in[at].wait()
-        whole_out[at].start()
-    vec, tall = r.vec_raw, r.tok_raw
+
+    widen(0)
+    widen(1)
+    tok_load.wait()
+    vec_load.wait()
+    vec, tall = r.vec, r.tall
     width = r.ln1_gain.shape[1]
-    for at, done in enumerate((r.ln1_gain, r.ln1_bias, r.ln2_gain, r.ln2_bias, r.chan_out_bias)):
+    half = vec.shape[1]
+    r.out_tok_in[...] = tall[pl.ds(0, rows)][:count].astype(F32)
+    r.out_tok_out[...] = tall[pl.ds(rows, rows)][:count].astype(F32)
+    outs = (r.out_ln1_gain, r.out_ln1_bias, r.out_ln2_gain, r.out_ln2_bias, r.out_chan_out_bias)
+    for at, done in enumerate(outs):
         done[...] = vec[pl.ds(at, 1), :][:, :width]
-    half = vec.shape[1]
     for at in range(r.chan_in_bias.shape[0]):
         row, lane = divmod(at * LANE, half)
-        r.chan_in_bias[pl.ds(at, 1), :] = vec[pl.ds(8 + row, 1), pl.ds(lane, LANE)]
+        r.out_chan_in_bias[pl.ds(at, 1), :] = vec[pl.ds(8 + row, 1), pl.ds(lane, LANE)]
     for at in range(toks // LANE):
-        r.tok_in_bias[pl.ds(at, 1), :] = vec[pl.ds(16, 1), pl.ds(at * LANE, LANE)]
-    r.tok_out_bias[...] = vec[pl.ds(24, 1), :][:, :count]
-    r.tok_in[...] = tall[pl.ds(0, rows)][:count].astype(F32)
-    r.tok_out[...] = tall[pl.ds(rows, rows)][:count].astype(F32)
-    for copy in stores + whole_out:
-        copy.wait()
+        r.out_tok_in_bias[pl.ds(at, 1), :] = vec[pl.ds(16, 1), pl.ds(at * LANE, LANE)]
+    r.out_tok_out_bias[...] = vec[pl.ds(24, 1), :][:, :count]
+    for store in small_stores:
+        store.start()
+    for at in range(2, len(loads)):
+        widen(at)
+    for load, store in zip(images_in, images_out):
+        load.wait()
+        store.start()
+    for store in stores + images_out + small_stores:
+        store.wait()
 
 
 def finish(out, count, width):
     full, hidden = out.g_chan_in.shape
-    toks = out.tall.shape[1]
+    toks = out.tok_grads.shape[1]
     hbm = pl.BlockSpec(memory_space=pl.ANY)
-    inside = pl.BlockSpec(memory_space=pltpu.VMEM)
     arrays = dict(
         mixed_raw=out.mixed,
         gin_raw=out.gin,
         chan_in_raw=out.g_chan_in,
         chan_out_raw=out.g_chan_out,
-        tok_raw=out.tall,
-        vec_raw=out.vec_out,
+        tok_raw=out.tok_grads,
+        vec_raw=out.vec_grads,
     )
     outs = dict(
         mixed=(out.mixed.shape, BF),
         gin=(out.gin.shape, BF),
         chan_in=((full, hidden), F32),
         chan_out=((hidden, full), F32),
+        tok_in=((count, toks), F32),
+        tok_out=((count, toks), F32),
         ln1_gain=((1, width), F32),
         ln1_bias=((1, width), F32),
         ln2_gain=((1, width), F32),
@@ -1108,22 +1156,25 @@
         chan_in_bias=((hidden // LANE, LANE), F32),
         tok_in_bias=((toks // LANE, LANE), F32),
         tok_out_bias=((1, count), F32),
-        tok_in=((count, toks), F32),
-        tok_out=((count, toks), F32),
     )
+    smalls = list(outs)[4:]
     parts = 4
     scratch = dict(
         pieces=pltpu.VMEM((2, parts, full // parts, hidden), BF),
         wide=pltpu.VMEM((2, parts, full // parts, hidden), F32),
         images=pltpu.VMEM((2,) + out.mixed.shape, BF),
-        sems=pltpu.SemaphoreType.DMA((10 + 4 * parts,)),
+        tall=pltpu.VMEM(out.tok_grads.shape, BF),
+        vec=pltpu.VMEM(out.vec_grads.shape, F32),
+        sems=pltpu.SemaphoreType.DMA((4 * parts + 10 + len(smalls),)),
     )
+    for name in smalls:
+        scratch["out_" + name] = pltpu.VMEM(*outs[name])
     names = list(arrays) + list(outs) + list(scratch)
     results = pl.pallas_call(
-        functools.partial(finish_kernel, names),
+        functools.partial(finish_kernel, names, smalls),
         out_shape=tuple(jax.ShapeDtypeStruct(*outs[name]) for name in outs),
-        in_specs=[hbm] * 4 + [inside] * 2,
-        out_specs=(hbm,) * 4 + (inside,) * 10,
+        in_specs=[hbm] * len(arrays),
+        out_specs=(hbm,) * len(outs),
         scratch_shapes=list(scratch.values()),
         compiler_params=pltpu.CompilerParams(vmem_limit_bytes=63 * 2**20),
         name="finish",

time: 130 us -> 124 us (0.954)
  Pallas kernels: 128 us -> 123 us
    pallas_call x1, Pallas kernels: 122 us -> 118 us  [run_layer(): pl.pallas_call(functools.partial(layer_kernel, cfg, names), out_shape=tup...]
where the time goes in v4:
time: 124 us
  Pallas kernels  123 us (99%)
  between operations  1.46 us (1%)
    pallas_call x1, Pallas kernels, run_layer(): pl.pallas_call(functools.partial(layer_kernel, cfg, names), out_shape=tup...  118 us
    pallas_call x1, Pallas kernels, finish(): pl.pallas_call(functools.partial(finish_kernel, names, smalls), out_shape...  4.9 us

profile of v4, /device:TPU:0, one launch (start us, length us, event | category | flops | bytes accessed | tf_op | source)
XLA Modules:
  0.0 124.2 jit_solution(3449660828813506422)
XLA Ops:
  1.3 117.9 %mixer_layer.1 = (bf16[12,192,196]{2,1,0:T(8,128)(2,1)}, bf16[12,192,196]{2,1,0:T(8,128)(2,1)}, bf16[448,384]{1,0:T(8,128)(2,1)}, f32[32,384]{1,0:T(8,128)}, bf1...) custom-call(s32[1]{0:T(128)S(6)} %copy.29.refs_0_, bf16[12,192,196]{2,1,0:T(8,128)(2,1)} %bitcast.22, ...), custom_call_target="tpu_custom_call" | custom-call | tf_op jit(solution)/shard_map/mixer_layer/pallas_call | solution.py:1052
  119.2 4.9 %finish.1 = (bf16[12,192,196]{2,1,0:T(8,128)(2,1)}, bf16[12,192,196]{2,1,0:T(8,128)(2,1)}, f32[768,768]{1,0:T(8,128)}, f32[768,768]{1,0:T(8,128)}, f32[196,384]{...) custom-call(bf16[12,192,196]{2,1,0:T(8,128)(2,1)} %get-tuple-element, ...), custom_call_target="tpu_custom_call" | custom-call | tf_op jit(solution)/shard_map/finish/pallas_call | solution.py:1173

commit v5 on v4

--- a/solution.py
+++ b/solution.py
@@ -340,7 +340,7 @@
                     o_mirror_back(k).wait_recv()
                     o_fold_rest(k).start()
 
-        e_at = (1, 2, 3, 4, 6)
+        e_at = (0, 1, 2, 3, 5)
         o_at = (1, 3, 5, 6, 7)
 
         def o_first(k):

time: 124 us -> 124 us (level)
  no operation moved by 1% of the time
where the time goes in v5:
time: 124 us; the launch traced here: 123 us
  Pallas kernels  122 us (98%)
  between operations  1.46 us (1%)
    pallas_call x1, Pallas kernels, run_layer(): pl.pallas_call(functools.partial(layer_kernel, cfg, names), out_shape=tup...  117 us
    pallas_call x1, Pallas kernels, finish(): pl.pallas_call(functools.partial(finish_kernel, names, smalls), out_shape...  4.9 us

profile of v5, /device:TPU:0, one launch (start us, length us, event | category | flops | bytes accessed | tf_op | source)
XLA Modules:
  0.0 123.4 jit_solution(18313173052256301321)
XLA Ops:
  1.3 117.0 %mixer_layer.1 = (bf16[12,192,196]{2,1,0:T(8,128)(2,1)}, bf16[12,192,196]{2,1,0:T(8,128)(2,1)}, bf16[448,384]{1,0:T(8,128)(2,1)}, f32[32,384]{1,0:T(8,128)}, bf1...) custom-call(s32[1]{0:T(128)S(6)} %copy.29.refs_0_, bf16[12,192,196]{2,1,0:T(8,128)(2,1)} %bitcast.22, ...), custom_call_target="tpu_custom_call" | custom-call | tf_op jit(solution)/shard_map/mixer_layer/pallas_call | solution.py:1052
  118.3 4.9 %finish.1 = (bf16[12,192,196]{2,1,0:T(8,128)(2,1)}, bf16[12,192,196]{2,1,0:T(8,128)(2,1)}, f32[768,768]{1,0:T(8,128)}, f32[768,768]{1,0:T(8,128)}, f32[196,384]{...) custom-call(bf16[12,192,196]{2,1,0:T(8,128)(2,1)} %get-tuple-element, ...), custom_call_target="tpu_custom_call" | custom-call | tf_op jit(solution)/shard_map/finish/pallas_call | solution.py:1173
